TPU v7x, 32 devices: a whole 2x2x4 slice. The times are simulated.
32 devices in a mesh: dp: 4 (over y, x), seq: 8 (over z, core).
Axes of the slice: x: 2, y: 2, z: 4, core: 2. Of those that a mesh axis runs over, the one named last changes fastest.
Arguments:
- tokens: bfloat16 [16384, 1024], P(('dp', 'seq')), may hold values from -6 to 6
- doc_lengths: int32 [4, 3], P('dp'), may hold values from 1 to 4094, as said below
- norm_gain: bfloat16 [1024], replicated, may hold values from 0.5 to 1.5
- w_qkv: bfloat16 [1024, 3072], P(('dp', 'seq')), may hold values from -0.1875 to 0.1875
- w_beta: bfloat16 [1024, 8], P(('dp', 'seq')), may hold values from -0.375 to 0.375
- conv_weight: bfloat16 [4, 3072], replicated, may hold values from -3 to 3
- head_gain: bfloat16 [128], replicated, may hold values from 0.5 to 1.5
- w_out: bfloat16 [1024, 1024], P(('dp', 'seq')), may hold values from -0.1875 to 0.1875
- mlp_gain: bfloat16 [1024], replicated, may hold values from 0.5 to 1.5
- w_mlp_in: bfloat16 [1024, 5632], P(('dp', 'seq')), may hold values from -0.1875 to 0.1875
- w_down: bfloat16 [2816, 1024], P(('dp', 'seq')), may hold values from -0.109375 to 0.109375
- grad_out: bfloat16 [16384, 1024], P(('dp', 'seq')), may hold values from -6 to 6
Outputs:
- out: bfloat16 [16384, 1024], P(('dp', 'seq'))
- grad_tokens: bfloat16 [16384, 1024], P(('dp', 'seq'))
- grad_norm_gain: float32 [1024], replicated
- grad_w_qkv: float32 [1024, 3072], P(('dp', 'seq'))
- grad_w_beta: float32 [1024, 8], P(('dp', 'seq'))
- grad_conv: float32 [4, 3072], replicated
- grad_head_gain: float32 [128], replicated
- grad_w_out: float32 [1024, 1024], P(('dp', 'seq'))
- grad_mlp_gain: float32 [1024], replicated
- grad_w_mlp_in: float32 [1024, 5632], P(('dp', 'seq'))
- grad_w_down: float32 [2816, 1024], P(('dp', 'seq'))
Inputs may be any that keep to these rules, and one draw needn't show every extreme that they name: `doc_lengths`: each row holds, in order, the lengths of the three documents packed into one group's 4096 tokens; the first and the last are each shorter than 512.
All inputs are finite; a program needn't handle non-finite values.
Results may differ from a plain program's by a relative error of at most 0.015.
Values may be sent and summed in bfloat16 or wider, within the bound.
A program may use at most 320 MiB of HBM per device.

v0:
```python
import functools

import jax
import jax.numpy as jnp
from jax import lax
from jax.experimental import pallas as pl
from jax.experimental.pallas import tpu as pltpu
from jax.sharding import PartitionSpec as P

norm_eps = 1e-05
unit_eps = 1e-06
MESH = pl.DeviceIdType.MESH
f32, bf16 = jnp.float32, jnp.bfloat16
HIGH = lax.Precision.HIGH
VMEM_LIMIT = 56 << 20


def nn(a, b, prec=None):
    return lax.dot_general(a, b, (((1,), (0,)), ((), ())), precision=prec, preferred_element_type=f32)


def nt(a, b, prec=None):
    return lax.dot_general(a, b, (((1,), (1,)), ((), ())), precision=prec, preferred_element_type=f32)


def tn(a, b, prec=None):
    return lax.dot_general(a, b, (((0,), (0,)), ((), ())), precision=prec, preferred_element_type=f32)


def unit_lower_inverses(mats, row, col):
    size = mats[0].shape[0]
    block = min(8, size)
    eye = (row == col).astype(f32)
    near = row // block == col // block
    powers = [jnp.where(near, -a, 0.0) for a in mats]
    inverses = [eye + p for p in powers]
    reach = 2
    while reach < block:
        powers = [nn(p, p, HIGH) for p in powers]
        inverses = [t + nn(t, p, HIGH) for t, p in zip(inverses, powers)]
        reach *= 2
    while block < size:
        pairs = size // (2 * block)

        def lower(m, block=block, pairs=pairs):
            return jnp.concatenate([m[(2 * i + 1) * block : (2 * i + 2) * block] for i in range(pairs)], axis=0)

        def spread(m, fill, block=block, pairs=pairs):
            return jnp.concatenate(
                [x for i in range(pairs) for x in (fill[2 * i * block : (2 * i + 1) * block], m[i * block : (i + 1) * block])],
                axis=0,
            )

        off = (row // (2 * block) == col // (2 * block)) & (row // block == col // block + 1)
        lows = [lower(jnp.where(off, a, 0.0)) for a in mats]
        crossed = [nn(x, t, HIGH) for x, t in zip(lows, inverses)]
        zero = jnp.zeros((size, size), f32)
        below = [lower(t) for t in inverses]
        fixed = [x - nn(x, spread(y, zero), HIGH) for x, y in zip(below, crossed)]
        inverses = [spread(x, t) for x, t in zip(fixed, inverses)]
        block *= 2
    return inverses


def head_column(matrix, head):
    lane = lax.broadcasted_iota(jnp.int32, matrix.shape, 1)
    return jnp.sum(jnp.where(lane == head, matrix, 0.0), axis=1, keepdims=True)


def masks_of(docs_col, docs_row):
    size = docs_col.shape[0]
    row = lax.broadcasted_iota(jnp.int32, (size, size), 0)
    col = lax.broadcasted_iota(jnp.int32, (size, size), 1)
    same = docs_col == docs_row
    return row, col, same


def local_kernel(
    sizes, chunk, gathers, *refs,
):
    local_body(sizes, chunk, gathers, refs[:gathers], *refs[gathers:])


def local_body(
    sizes, chunk, gathers, shards, pq, pk, pv, hq, hk, hv, tq, tk, tv, aux, docs_c, docs_r, logits,
    cq, ck, cv, w_o, u_o, qt_o, o_o, t_o, p_o, kk_o, dt_o, ft_o, map_o, turned_o, add_o, *rest,
):
    head = pl.program_id(0)
    pad = rest[gathers]
    gather_beside(sizes, head, shards, rest[:gathers], rest[gathers + 1 :])
    rows, width = pq.shape
    keeps = (aux[:, 2:3], aux[:, 3:4], aux[:, 4:5])
    acts = []
    for src, halo, taps, dst in ((pq, hq, tq, cq), (pk, hk, tk, ck), (pv, hv, tv, cv)):
        pad[0:8, :] = halo[...]
        pad[8 : 8 + rows, :] = src[...]
        conv = taps[3:4, :] * src[...]
        for back in (1, 2, 3):
            conv = conv + taps[3 - back : 4 - back, :] * (pad[8 - back : 8 - back + rows, :] * keeps[back - 1])
        dst[...] = conv
        acts.append(conv * jax.nn.sigmoid(conv))
    q = acts[0] * (lax.rsqrt(jnp.sum(acts[0] * acts[0], axis=1, keepdims=True) + unit_eps) * width ** (-0.5))
    k = acts[1] * lax.rsqrt(jnp.sum(acts[1] * acts[1], axis=1, keepdims=True) + unit_eps)
    v = acts[2]
    beta = jax.nn.sigmoid(head_column(logits[...], head))
    cont, last = aux[:, 0:1], aux[:, 1:2]
    n_chunk = rows // chunk
    cuts = [slice(c * chunk, (c + 1) * chunk) for c in range(n_chunk)]
    row = lax.broadcasted_iota(jnp.int32, (chunk, chunk), 0)
    col = lax.broadcasted_iota(jnp.int32, (chunk, chunk), 1)
    same = [docs_c[sl, :] == docs_r[:, sl] for sl in cuts]
    kks = [nt(k[sl], k[sl], HIGH) for sl in cuts]
    ps = [jnp.where(m & (row >= col), nt(q[sl], k[sl], HIGH), 0.0) for m, sl in zip(same, cuts)]
    ts = unit_lower_inverses(
        [jnp.where(m & (row > col), beta[sl] * kk, 0.0) for m, sl, kk in zip(same, cuts, kks)], row, col
    )
    rhs = [jnp.concatenate([(beta[sl] * cont[sl]) * k[sl], beta[sl] * v[sl]], axis=1) for sl in cuts]
    wus = [nn(t, r, HIGH) for t, r in zip(ts, rhs)]
    pwus = [nn(p, wu, HIGH) for p, wu in zip(ps, wus)]
    xs = [tn(last[sl] * k[sl], wu, HIGH) for sl, wu in zip(cuts, wus)]
    d_row = lax.broadcasted_iota(jnp.int32, (width, width), 0)
    d_col = lax.broadcasted_iota(jnp.int32, (width, width), 1)
    seg = None
    for c, sl in enumerate(cuts):
        cc = cont[sl]
        dt = jnp.where(d_row == d_col, cc[chunk - 1 : chunk], 0.0) - xs[c][:, :width]
        ft = xs[c][:, width:]
        w_o[sl, :] = wus[c][:, :width]
        u_o[sl, :] = wus[c][:, width:]
        qt_o[sl, :] = cc * q[sl] - pwus[c][:, :width]
        o_o[sl, :] = pwus[c][:, width:]
        t_o[sl, :] = ts[c]
        p_o[sl, :] = ps[c]
        kk_o[sl, :] = kks[c]
        dt_o[c * width : (c + 1) * width, :] = dt
        ft_o[c * width : (c + 1) * width, :] = ft
        if seg is None:
            seg = jnp.concatenate([dt, ft], axis=1)
        else:
            seg = nn(dt, seg, HIGH)
            seg = jnp.concatenate([seg[:, :width], seg[:, width:] + ft], axis=1)
    map_o[0] = seg[:, :width]
    turned_o[0] = seg[:, :width].T
    add_o[0] = seg[:, width:]


def relay_kernel(n_seq, back, map_ref, add_ref, out_ref, send, ssem, rsem):
    d, s = lax.axis_index("dp"), lax.axis_index("seq")
    heads = map_ref.shape[0]
    if back:
        first, final = s == n_seq - 1, s == 0
        ahead, behind = s - 1, s + 1
    else:
        first, final = s == 0, s == n_seq - 1
        ahead, behind = s + 1, s - 1
    barrier = pltpu.get_barrier_semaphore()

    @pl.when(jnp.logical_not(first))
    def _():
        pl.semaphore_signal(barrier, inc=1, device_id=(d, behind), device_id_type=MESH)

    @pl.when(jnp.logical_not(final))
    def _():
        pl.semaphore_signal(barrier, inc=1, device_id=(d, ahead), device_id_type=MESH)

    pl.semaphore_wait(barrier, jnp.where(first | final, 1, 2))

    def copy_of(h):
        return pltpu.make_async_remote_copy(
            src_ref=send.at[h], dst_ref=out_ref.at[h], send_sem=ssem.at[h], recv_sem=rsem.at[h],
            device_id=(d, ahead), device_id_type=MESH,
        )

    @pl.when(first)
    def _():
        def start(h, carry):
            out_ref[h] = jnp.zeros(out_ref.shape[1:], out_ref.dtype)
            send[h] = add_ref[h].astype(bf16)
            copy_of(h).start()
            return carry

        lax.fori_loop(0, heads, start, 0)

    @pl.when(jnp.logical_not(first))
    def _():
        def step(h, carry):
            copy_of(h).wait_recv()

            @pl.when(jnp.logical_not(final))
            def _():
                send[h] = (nn(map_ref[h], out_ref[h].astype(f32), HIGH) + add_ref[h]).astype(bf16)
                copy_of(h).start()

            return carry

        lax.fori_loop(0, heads, step, 0)

    @pl.when(jnp.logical_not(final))
    def _():
        def sent(h, carry):
            copy_of(h).wait_send()
            return carry

        lax.fori_loop(0, heads, sent, 0)


def output_kernel(chunk, zin, dt, ft, qt, o0, gain, z_o, o_o, head_o):
    rows, width = qt.shape
    z = zin[0].astype(f32)
    for c in range(rows // chunk):
        sl = slice(c * chunk, (c + 1) * chunk)
        ds = slice(c * width, (c + 1) * width)
        z_o[ds, :] = z
        o = o0[sl, :] + nn(qt[sl, :], z, HIGH)
        o_o[sl, :] = o
        scale = lax.rsqrt(jnp.mean(o * o, axis=1, keepdims=True) + norm_eps)
        head_o[sl, :] = (o * scale * gain[...]).astype(bf16)
        if c + 1 < rows // chunk:
            z = nn(dt[ds, :], z, HIGH) + ft[ds, :]


def seed_kernel(chunk, dh, o, gain, qt, dt, do_o, b_o, seed_o, dgain_o):
    head = pl.program_id(0)
    rows, width = qt.shape
    ov, dhv = o[...], dh[...]
    scale = lax.rsqrt(jnp.mean(ov * ov, axis=1, keepdims=True) + norm_eps)
    n = ov * scale
    dg = jnp.sum(dhv * n, axis=0, keepdims=True)
    dgain_o[...] = jnp.where(head == 0, 0.0, dgain_o[...]) + jnp.broadcast_to(dg, dgain_o.shape)
    y = dhv * gain[...]
    do = (y - n * jnp.mean(y * n, axis=1, keepdims=True)) * scale
    do_o[...] = do
    g = None
    for c in reversed(range(rows // chunk)):
        sl = slice(c * chunk, (c + 1) * chunk)
        ds = slice(c * width, (c + 1) * width)
        b_o[ds, :] = tn(qt[sl, :], do[sl], HIGH)
        g = b_o[ds, :] if g is None else tn(dt[ds, :], g, HIGH) + b_o[ds, :]
    seed_o[0] = g


def back_kernel(
    chunk, pq, pk, pv, hq, hk, hv, tq, tk, tv, aux, docs_c, docs_r, logits,
    cq, ck, cv, w_r, u_r, t_r, p_r, kk_r, z_r, do_r, dt_r, b_r, g_r,
    dpq, dpk, dpv, dhq, dhk, dhv, dtq, dtk, dtv, dlogit_o, pad, mask1, mask2, mask3,
):
    head = pl.program_id(0)
    rows, width = pq.shape
    cont, last = aux[:, 0:1], aux[:, 1:2]
    keeps = (aux[:, 2:3], aux[:, 3:4], aux[:, 4:5])
    scale = width ** (-0.5)
    beta = jax.nn.sigmoid(head_column(logits[...], head))
    sq, sk, sv = (jax.nn.sigmoid(x[...]) for x in (cq, ck, cv))
    aq, ak, v = cq[...] * sq, ck[...] * sk, cv[...] * sv
    iq = lax.rsqrt(jnp.sum(aq * aq, axis=1, keepdims=True) + unit_eps)
    ik = lax.rsqrt(jnp.sum(ak * ak, axis=1, keepdims=True) + unit_eps)
    uq, k = aq * iq, ak * ik
    q = uq * scale
    g = g_r[0].astype(f32)
    dqs, dks, dvs, dbs = [], [], [], []
    for c in reversed(range(rows // chunk)):
        sl = slice(c * chunk, (c + 1) * chunk)
        ds = slice(c * width, (c + 1) * width)
        row, col, same = masks_of(docs_c[sl, :], docs_r[:, sl])
        qc, kc, vc, bc, cc, lc = q[sl], k[sl], v[sl], beta[sl], cont[sl], last[sl]
        z = z_r[ds, :]
        do = do_r[sl, :]
        wkz = nn(jnp.concatenate([w_r[sl, :], kc], axis=0), z)
        u = u_r[sl, :] - wkz[:chunk]
        kz = wkz[chunk:]
        du = tn(p_r[sl, :], do) + nn(lc * kc, g)
        dr = tn(t_r[sl, :], du)
        y = nt(jnp.concatenate([do, dr], axis=0), jnp.concatenate([u, z], axis=0))
        dp = jnp.where(same & (row >= col), y[:chunk, :chunk], 0.0)
        da = jnp.where(same & (row > col), -y[chunk:, :chunk], 0.0)
        bda = bc * da
        pak = nn(jnp.concatenate([dp, bda], axis=0), kc)
        dqs.append(cc * y[:chunk, chunk:] + pak[:chunk])
        dks.append(
            tn(jnp.concatenate([dp, bda], axis=0), jnp.concatenate([qc, kc], axis=0))
            + pak[chunk:] + lc * nt(u, g) - (bc * cc) * y[chunk:, chunk:]
        )
        dvs.append(bc * dr)
        dbs.append(
            jnp.sum(dr * (vc - cc * kz), axis=1, keepdims=True)
            + jnp.sum(da * kk_r[sl, :], axis=1, keepdims=True)
        )
        if c > 0:
            g = tn(dt_r[ds, :], g) + b_r[ds, :]
    dq, dk, dv, db = (jnp.concatenate(x[::-1], axis=0) for x in (dqs, dks, dvs, dbs))
    lane = lax.broadcasted_iota(jnp.int32, dlogit_o.shape, 1)
    dlogit_o[...] = jnp.where(lane == head, db * beta * (1.0 - beta), jnp.where(head == 0, 0.0, dlogit_o[...]))
    du_q = dq * scale
    da_q = (du_q - uq * jnp.sum(uq * du_q, axis=1, keepdims=True)) * iq
    da_k = (dk - k * jnp.sum(k * dk, axis=1, keepdims=True)) * ik
    for dact, sg, c_r, src, halo, taps, dst, dhalo, dtaps in (
        (da_q, sq, cq, pq, hq, tq, dpq, dhq, dtq),
        (da_k, sk, ck, pk, hk, tk, dpk, dhk, dtk),
        (dv, sv, cv, pv, hv, tv, dpv, dhv, dtv),
    ):
        dconv = dact * (sg * (1.0 + c_r[...] * (1.0 - sg)))
        pad[0:8, :] = halo[...]
        pad[8 : 8 + rows, :] = src[...]
        zero = jnp.zeros((8, width), f32)
        total = taps[3:4, :] * dconv
        early = zero
        gtaps = [None] * 4
        gtaps[3] = jnp.sum(dconv * src[...], axis=0, keepdims=True)
        for back, mask in ((1, mask1), (2, mask2), (3, mask3)):
            kept = dconv * keeps[back - 1]
            gtaps[3 - back] = jnp.sum(kept * pad[8 - back : 8 - back + rows, :], axis=0, keepdims=True)
            mask[0:8, :] = zero
            mask[8 : 8 + rows, :] = kept
            mask[8 + rows : 16 + rows, :] = zero
            total = total + taps[3 - back : 4 - back, :] * mask[8 + back : 8 + back + rows, :]
            early = early + taps[3 - back : 4 - back, :] * mask[back : back + 8, :]
        dst[...] = total
        dhalo[...] = early
        dtaps[...] = jnp.concatenate(gtaps + [jnp.zeros((4, width), f32)], axis=0)


def bit_orders(n_dp, n_seq):
    dp_bits = [("dp", i) for i in range(n_dp.bit_length() - 1)]
    seq_bits = [("seq", i) for i in range(n_seq.bit_length() - 1)]
    return (
        seq_bits[:1] + dp_bits + seq_bits[1:],
        seq_bits[:1] + dp_bits[::-1] + seq_bits[1:],
        seq_bits + dp_bits,
        seq_bits + dp_bits[::-1],
    )


def scatter_kernel(n_dp, n_seq, units, slots, n_left, n_right, n_out, *refs):
    lefts = refs[:n_left]
    rights = refs[n_left : n_left + n_right]
    small_in = refs[n_left + n_right]
    outs = refs[n_left + n_right + 1 : n_left + n_right + 1 + n_out]
    small_out = refs[n_left + n_right + 1 + n_out]
    scratch = list(refs[n_left + n_right + 2 + n_out :])
    orders = bit_orders(n_dp, n_seq)
    steps = len(orders[0])
    pool = [scratch.pop(0) for _ in range(2 * (1 + max(slots)))]
    own = [pool[2 * slots[u] + half] for u in range(len(units)) for half in (0, 1)]
    before = [max([w for w in range(u) if slots[w] == slots[u]], default=None) for u in range(len(units))]
    got = [[scratch.pop(0) for _ in range(steps)] for _ in range(2 * len(units))]
    small_got, ssem, rsem, small_ssem, small_rsem = scratch
    index = {"dp": lax.axis_index("dp"), "seq": lax.axis_index("seq")}

    def bit_of(axis, bit):
        return (index[axis] // 2**bit) % 2

    def partner(axis, bit):
        other = dict(index)
        other[axis] = index[axis] + (1 - 2 * bit_of(axis, bit)) * 2**bit
        return (other["dp"], other["seq"])

    barrier = pltpu.get_barrier_semaphore()
    for axis, bit in orders[0]:
        pl.semaphore_signal(barrier, inc=1, device_id=partner(axis, bit), device_id_type=MESH)
    pl.semaphore_wait(barrier, steps)

    def weights(order):
        return {key: 2 ** (steps - 1 - i) for i, key in enumerate(order)}

    def place(order, axis, value):
        w = weights(order)
        return sum(((value // 2**b) % 2) * w[(a, b)] for a, b in order if a == axis)

    def compute(u):
        kind, li, ri, first, cols, _, _, first_order = units[u]
        left, right = lefts[li], rights[ri]
        block = left.shape[0] // (n_dp * n_seq)
        group = block * n_seq
        for half in (0, 1):
            order, buf = orders[first_order + half], own[2 * u + half]
            part = pl.ds(first + half * (cols // 2), cols // 2)

            def rows_of(m, carry):
                base = place(order, "dp", m)
                tile = nn(left[pl.ds(pl.multiple_of(m * group, 16), group), :], right[:, part])
                for j in range(n_seq):
                    piece = tile[j * block : (j + 1) * block]
                    if kind == "stack":
                        piece = jnp.concatenate([piece[:, : cols // 4], piece[:, cols // 4 :]], axis=0)
                    buf[base + place(order, "seq", j)] = piece.astype(bf16)
                return carry

            lax.fori_loop(0, n_dp, rows_of, 0)

    def copy_of(u, half, k):
        src = own[2 * u + half] if k == 0 else got[2 * u + half][k - 1]
        dst = got[2 * u + half][k]
        axis, bit = orders[units[u][7] + half][k]
        count = dst.shape[0]
        return pltpu.make_async_remote_copy(
            src_ref=src.at[pl.ds((1 - bit_of(axis, bit)) * count, count)], dst_ref=dst,
            send_sem=ssem.at[u, half, k], recv_sem=rsem.at[u, half, k],
            device_id=partner(axis, bit), device_id_type=MESH,
        )

    def merge(u, half, k):
        src = own[2 * u + half] if k == 0 else got[2 * u + half][k - 1]
        dst = got[2 * u + half][k]
        axis, bit = orders[units[u][7] + half][k]
        count = dst.shape[0]
        mine = bit_of(axis, bit) * count
        copy_of(u, half, k).wait_recv()
        if k < steps - 1:
            def add(i, carry):
                dst[i] = (dst[i].astype(f32) + src[mine + i].astype(f32)).astype(bf16)
                return carry

            lax.fori_loop(0, count, add, 0)
            copy_of(u, half, k + 1).start()
        else:
            kind, _, _, first, cols, oi, to, _ = units[u]
            total = dst[0].astype(f32) + src[mine].astype(f32)
            start, wide = to + half * (cols // 2), cols // 2
            if kind == "stack":
                block = total.shape[0] // 2
                outs[oi][:, start : start + wide // 2] = total[:block]
                outs[oi][:, start + wide // 2 : start + wide] = total[block:]
            else:
                outs[oi][:, start : start + wide] = total

    def small_copy(k):
        axis, bit = orders[0][k]
        return pltpu.make_async_remote_copy(
            src_ref=small_in if k == 0 else small_got.at[steps + k - 1], dst_ref=small_got.at[k],
            send_sem=small_ssem.at[k], recv_sem=small_rsem.at[k],
            device_id=partner(axis, bit), device_id_type=MESH,
        )

    def small_step(k):
        small_copy(k).wait_recv()
        mine = small_in[...] if k == 0 else small_got[steps + k - 1]
        if k < steps - 1:
            small_got[steps + k] = small_got[k] + mine
            small_copy(k + 1).start()
        else:
            small_out[...] = small_got[k] + mine

    small_copy(0).start()
    for t in range(len(units) + steps):
        if t < len(units):
            if before[t] is not None:
                for half in (0, 1):
                    copy_of(before[t], half, 0).wait_send()
            compute(t)
            for half in (0, 1):
                copy_of(t, half, 0).start()
        if t < steps:
            small_step(t)
        for k in range(steps):
            u = t - 1 - k
            if 0 <= u < len(units):
                for half in (0, 1):
                    merge(u, half, k)
    for k in range(steps):
        small_copy(k).wait_send()
        for u in range(len(units)):
            if k > 0 or u not in before:
                for half in (0, 1):
                    copy_of(u, half, k).wait_send()


def scatter_grads(mesh_sizes, products, small, cid):
    n_dp, n_seq = mesh_sizes
    n = n_dp * n_seq
    orders = bit_orders(n_dp, n_seq)
    steps = len(orders[0])
    lefts, rights, units, shapes, outs = [], [], [], [], []
    for oi, (left, right, kind, cols) in enumerate(products):
        block = left.shape[0] // n
        lefts.append(left)
        rights.append(right)
        outs.append(jax.ShapeDtypeStruct((block, right.shape[1]), f32))
        first = 0
        for wide, first_order in cols:
            units.append((kind, oi, oi, first, wide, oi, first, first_order))
            first += wide
            shapes.append((2 * block, wide // 4) if kind == "stack" else (block, wide // 2))
    pool, slots = [], []
    for u, shape in enumerate(shapes):
        alike = [i for i, kept in enumerate(pool) if kept == shape]
        if len(alike) < 3:
            slots.append(len(pool))
            pool.append(shape)
        else:
            used = [max(w for w in range(u) if slots[w] == i) for i in alike]
            slots.append(alike[used.index(min(used))])
    own = [pltpu.VMEM((n,) + s, bf16) for s in pool for _ in (0, 1)]
    got = [pltpu.VMEM((n >> (k + 1),) + s, bf16) for s in shapes for _ in (0, 1) for k in range(steps)]
    vmem = pl.BlockSpec(memory_space=pltpu.VMEM)
    sems = pltpu.SemaphoreType.DMA((len(units), 2, steps))
    results = pl.pallas_call(
        functools.partial(scatter_kernel, n_dp, n_seq, units, slots, len(lefts), len(rights), len(outs)),
        in_specs=[vmem] * (len(lefts) + len(rights) + 1),
        out_specs=[vmem] * (len(outs) + 1),
        out_shape=outs + [jax.ShapeDtypeStruct(small.shape, f32)],
        scratch_shapes=own + got + [
            pltpu.VMEM((2 * steps,) + small.shape, f32), sems, sems,
            pltpu.SemaphoreType.DMA((steps,)), pltpu.SemaphoreType.DMA((steps,)),
        ],
        compiler_params=pltpu.CompilerParams(collective_id=cid, has_side_effects=True, vmem_limit_bytes=63 << 20),
        name="scatter_grads",
    )(*lefts, *rights, small)
    return results[:-1], results[-1]


def gather_steps(sizes, shard, whole, own_sem, ssem, rsem):
    n_dp, n_seq = sizes
    index = {"dp": lax.axis_index("dp"), "seq": lax.axis_index("seq")}
    orders = [order[::-1] for order in bit_orders(n_dp, n_seq)[:2]]
    steps = len(orders[0])
    by_rows = shard.shape[0] % 32 == 0
    extent = shard.shape[0 if by_rows else 1] // 2

    def flipped(keys):
        other = dict(index)
        for axis, bit in keys:
            other[axis] = other[axis] + (1 - 2 * ((index[axis] // 2**bit) % 2)) * 2**bit
        return (other["dp"], other["seq"])

    def half_of(ref, half):
        part = pl.ds(half * extent, extent)
        return ref.at[part] if by_rows else ref.at[:, part]

    def copy_of(half, path, k):
        order = orders[half]
        dp, seq = flipped([order[i] for i in path])
        dst = half_of(whole.at[dp * n_seq + seq], half)
        code = sum(2**i for i in path) + 2**k
        return pltpu.make_async_remote_copy(
            src_ref=dst if path else half_of(shard, half), dst_ref=dst,
            send_sem=ssem.at[half, code], recv_sem=rsem.at[half, code],
            device_id=flipped([order[k]]), device_id_type=MESH,
        )

    paths = sorted(
        (tuple(i for i in range(steps) if code >> i & 1) for code in range(2**steps)), key=lambda p: (len(p), p)
    )
    keep = pltpu.make_async_copy(shard, whole.at[index["dp"] * n_seq + index["seq"]], own_sem)

    def greet():
        barrier = pltpu.get_barrier_semaphore()
        for key in orders[0]:
            pl.semaphore_signal(barrier, inc=1, device_id=flipped([key]), device_id_type=MESH)
        pl.semaphore_wait(barrier, steps)

    def level(hops):
        if hops == 0:
            keep.start()
        for path in paths:
            if len(path) == hops:
                for half in (0, 1):
                    if path:
                        copy_of(half, path[:-1], path[-1]).wait_recv()
                    for k in range((path[-1] if path else -1) + 1, steps):
                        copy_of(half, path, k).start()

    def finish():
        for path in paths:
            if path:
                for half in (0, 1):
                    copy_of(half, path[:-1], path[-1]).wait_send()
        keep.wait()

    return steps, greet, level, finish


def gather_kernel(sizes, shard, whole, *sems):
    steps, greet, level, finish = gather_steps(sizes, shard, whole, *sems)
    greet()
    for hops in range(steps + 1):
        level(hops)
    finish()


def gather_beside(sizes, turn, shards, wholes, sems):
    plans = [
        gather_steps(sizes, shard, whole, *sems[3 * i : 3 * i + 3])
        for i, (shard, whole) in enumerate(zip(shards, wholes))
    ]
    if not plans:
        return
    steps = plans[0][0]
    for hops in range(steps + 1):
        @pl.when(turn == hops)
        def _(hops=hops):
            if hops == 0:
                plans[0][1]()
            for plan in plans:
                plan[2](hops)

    @pl.when(turn == steps + 1)
    def _():
        for plan in plans:
            plan[3]()


def gather_sems(sizes):
    sems = pltpu.SemaphoreType.DMA((2, sizes[0] * sizes[1]))
    return [pltpu.SemaphoreType.DMA, sems, sems]


def whole_like(sizes, shard):
    return jax.ShapeDtypeStruct((sizes[0] * sizes[1],) + shard.shape, shard.dtype)


def flat_rows(whole):
    return whole.reshape((whole.shape[0] * whole.shape[1],) + whole.shape[2:])


def gather_rows(sizes, shard, cid):
    anywhere = pl.BlockSpec(memory_space=pl.ANY)
    whole = pl.pallas_call(
        functools.partial(gather_kernel, sizes),
        in_specs=[anywhere],
        out_specs=anywhere,
        out_shape=whole_like(sizes, shard),
        scratch_shapes=gather_sems(sizes),
        compiler_params=pltpu.CompilerParams(collective_id=cid, has_side_effects=True),
        name="gather_rows",
    )(shard)
    return flat_rows(whole)


def from_behind(value, axis, steps):
    count = lax.axis_size(axis)
    first, last = (max(0, -steps), min(count, count - steps))
    return lax.ppermute(value, axis, [(source, source + steps) for source in range(first, last)])


def rms_scale(values, gain):
    return values * lax.rsqrt(jnp.mean(values * values, axis=-1, keepdims=True) + norm_eps) * gain


def doc_ids(lengths, positions):
    ends = jnp.cumsum(lengths)
    inside = (positions[:, None] >= ends[None, :]).astype(jnp.int32)
    return jnp.where(positions >= 0, jnp.sum(inside, axis=1), -1)


def swiglu(gate_up):
    half = gate_up.shape[1] // 2
    return jax.nn.silu(gate_up[:, :half]) * gate_up[:, half:]


def contract_rows(left, right):
    return tn(left, right)


def contract_cols(left, right):
    return nt(left, right)


def local(
    n_dp, n_seq, tokens, doc_lengths, norm_gain, w_qkv, w_beta, conv_weight, head_gain, w_out, mlp_gain, w_mlp_in, w_down, grad_out,
):
    rows, model = tokens.shape
    heads = w_beta.shape[1]
    width = head_gain.shape[0]
    taps_n = conv_weight.shape[0]
    qkv = w_qkv.shape[1]
    chunk = min(128, rows)
    n_chunk = rows // chunk
    both = ("dp", "seq")

    sizes = (n_dp, n_seq)
    own_kernels = (model // (n_dp * n_seq)) % 32 == 0 and heads > (n_dp * n_seq).bit_length()
    w_m = lax.all_gather(w_mlp_in, both, axis=0, tiled=True)
    w_in = jnp.concatenate([w_qkv, jnp.pad(w_beta, ((0, 0), (0, 128 - heads)))], axis=1)
    if own_kernels:
        beside = [w_out, w_down]
        w_in = gather_rows(sizes, w_in, 3)
    else:
        beside = []
        w_in, w_o, w_d = (lax.all_gather(w, both, axis=0, tiled=True) for w in (w_in, w_out, w_down))

    inputs = tokens.astype(f32)
    norm_one, pull_one = jax.vjp(rms_scale, inputs, norm_gain.astype(f32))
    xn1 = norm_one.astype(bf16)
    projected = nn(xn1, w_in)
    logits = projected[:, qkv : qkv + heads]
    start = lax.axis_index("seq") * rows
    docs_pad = doc_ids(doc_lengths[0], start - taps_n + 1 + jnp.arange(rows + taps_n - 1, dtype=jnp.int32))
    docs = docs_pad[taps_n - 1 :]
    by_chunk = docs.reshape(n_chunk, chunk)
    before = docs_pad[taps_n - 2 : taps_n - 2 + rows].reshape(n_chunk, chunk)[:, :1]
    aux = jnp.stack(
        [(by_chunk == before).reshape(-1), (by_chunk == by_chunk[:, -1:]).reshape(-1)]
        + [docs_pad[taps_n - 1 - b : taps_n - 1 - b + rows] == docs for b in (1, 2, 3)]
        + [docs < -5] * 3,
        axis=1,
    ).astype(f32)
    docs_c, docs_r = docs[:, None], docs[None, :]
    received = from_behind(projected[rows - taps_n + 1 :, :qkv].astype(bf16), "seq", 1).astype(f32)
    halo = jnp.pad(received, ((8 - taps_n + 1, 0), (0, 0)))
    taps = jnp.pad(conv_weight.astype(f32), ((0, 8 - taps_n), (0, 0)))

    def third(block_rows):
        return [pl.BlockSpec((block_rows, width), lambda h, t=t: (0, t * heads + h)) for t in range(3)]

    def per_head(block_rows):
        return pl.BlockSpec((block_rows, width), lambda h: (0, h))

    def whole(shape):
        return pl.BlockSpec(shape, lambda h: (0,) * len(shape))

    state_block = pl.BlockSpec((1, width, width), lambda h: (h, 0, 0))
    params = pltpu.CompilerParams(vmem_limit_bytes=VMEM_LIMIT, dimension_semantics=("arbitrary",))
    cols = heads * width
    token_like = jax.ShapeDtypeStruct((rows, cols), f32)
    chunk_like = jax.ShapeDtypeStruct((rows, heads * chunk), f32)
    state_like = jax.ShapeDtypeStruct((n_chunk * width, cols), f32)
    common_specs = (
        third(rows) + third(8) + third(8)
        + [whole((rows, 8)), whole((rows, 1)), whole((1, rows)), whole((rows, heads))]
    )
    common = (projected,) * 3 + (halo,) * 3 + (taps,) * 3 + (aux, docs_c, docs_r, logits)
    chunk_block = pl.BlockSpec((rows, chunk), lambda h: (0, h))
    anywhere = pl.BlockSpec(memory_space=pl.ANY)
    maps_like = jax.ShapeDtypeStruct((heads, width, width), f32)
    cq, ck, cv, w_s, u_s, qt, o0, t_s, p_s, kk_s, dt, ft, seg_map, seg_turned, seg_add, *wholes = pl.pallas_call(
        functools.partial(local_kernel, sizes, chunk, len(beside)),
        grid=(heads,),
        in_specs=[anywhere] * len(beside) + common_specs,
        out_specs=[per_head(rows)] * 7 + [chunk_block] * 3 + [per_head(n_chunk * width)] * 2 + [state_block] * 3
        + [anywhere] * len(beside),
        out_shape=[token_like] * 7 + [chunk_like] * 3 + [state_like] * 2 + [maps_like] * 3
        + [whole_like(sizes, w) for w in beside],
        scratch_shapes=[pltpu.VMEM((rows + 8, width), f32)] + [sem for _ in beside for sem in gather_sems(sizes)],
        compiler_params=pltpu.CompilerParams(
            vmem_limit_bytes=VMEM_LIMIT, dimension_semantics=("arbitrary",),
            **(dict(collective_id=4, has_side_effects=True) if beside else {}),
        ),
        name="delta_local",
    )(*beside, *common)
    if beside:
        w_o, w_d = (flat_rows(w) for w in wholes)

    def relay(back, maps, adds, cid):
        return pl.pallas_call(
            functools.partial(relay_kernel, n_seq, back),
            in_specs=[pl.BlockSpec(memory_space=pltpu.VMEM)] * 2,
            out_specs=pl.BlockSpec(memory_space=pltpu.VMEM),
            out_shape=jax.ShapeDtypeStruct((heads, width, width), bf16),
            scratch_shapes=[
                pltpu.VMEM((heads, width, width), bf16),
                pltpu.SemaphoreType.DMA((heads,)),
                pltpu.SemaphoreType.DMA((heads,)),
            ],
            compiler_params=pltpu.CompilerParams(collective_id=cid, has_side_effects=True, vmem_limit_bytes=VMEM_LIMIT),
            name="relay_back" if back else "relay",
        )(maps, adds)

    state_in = relay(False, seg_map, seg_add, 0)
    gain_h = head_gain.astype(f32)[None, :]
    z_s, mixed, head_out = pl.pallas_call(
        functools.partial(output_kernel, chunk),
        grid=(heads,),
        in_specs=[state_block, per_head(n_chunk * width), per_head(n_chunk * width), per_head(rows), per_head(rows), whole((1, width))],
        out_specs=[per_head(n_chunk * width), per_head(rows), per_head(rows)],
        out_shape=[state_like, token_like, jax.ShapeDtypeStruct((rows, cols), bf16)],
        compiler_params=params,
        name="delta_out",
    )(state_in, dt, ft, qt, o0, gain_h)

    hidden_one = inputs + nn(head_out, w_o)
    norm_two, pull_two = jax.vjp(rms_scale, hidden_one, mlp_gain.astype(f32))
    xn2 = norm_two.astype(bf16)
    gate_up = nn(xn2, w_m)
    hidden_f, pull_act = jax.vjp(swiglu, gate_up)
    hidden = hidden_f.astype(bf16)
    out = (hidden_one + nn(hidden, w_d)).astype(bf16)

    grad_in = grad_out.astype(f32)
    d_hidden = contract_cols(grad_out, w_d)
    d_gate_up = pull_act(d_hidden)[0].astype(bf16)
    d_from_two, d_mlp_gain = pull_two(contract_cols(d_gate_up, w_m))
    d_hidden_one = grad_in + d_from_two
    d_att = d_hidden_one.astype(bf16)
    d_head = contract_cols(d_att, w_o)

    do, b_s, seed, d_head_gain = pl.pallas_call(
        functools.partial(seed_kernel, chunk),
        grid=(heads,),
        in_specs=[per_head(rows), per_head(rows), whole((1, width)), per_head(rows), per_head(n_chunk * width)],
        out_specs=[per_head(rows), per_head(n_chunk * width), state_block, whole((8, width))],
        out_shape=[token_like, state_like, jax.ShapeDtypeStruct((heads, width, width), f32), jax.ShapeDtypeStruct((8, width), f32)],
        compiler_params=params,
        name="delta_seed",
    )(d_head, mixed, gain_h, qt, dt)
    grad_end = relay(True, seg_turned, seed, 1)
    outs = pl.pallas_call(
        functools.partial(back_kernel, chunk),
        grid=(heads,),
        in_specs=common_specs + [per_head(rows)] * 5 + [chunk_block] * 3
        + [per_head(n_chunk * width), per_head(rows), per_head(n_chunk * width), per_head(n_chunk * width), state_block],
        out_specs=[per_head(rows)] * 3 + [per_head(8)] * 6 + [whole((rows, heads))],
        out_shape=[token_like] * 3 + [jax.ShapeDtypeStruct((8, cols), f32)] * 6 + [jax.ShapeDtypeStruct((rows, heads), f32)],
        scratch_shapes=[pltpu.VMEM((rows + 8, width), f32)] + [pltpu.VMEM((rows + 16, width), f32)] * 3,
        compiler_params=params,
        name="delta_back",
    )(*common, cq, ck, cv, w_s, u_s, t_s, p_s, kk_s, z_s, do, dt, b_s, grad_end)
    d_main = jnp.concatenate(outs[:3], axis=1)
    d_early = jnp.concatenate(outs[3:6], axis=1)
    d_conv = jnp.concatenate(outs[6:9], axis=1)[:taps_n]
    d_logits = outs[9]
    returned = from_behind(d_early[8 - taps_n + 1 :].astype(bf16), "seq", -1).astype(f32)
    d_projected = d_main + jnp.pad(returned, ((rows - taps_n + 1, 0), (0, 0)))
    d_proj_b = jnp.concatenate(
        [d_projected.astype(bf16), jnp.pad(d_logits.astype(bf16), ((0, 0), (0, 128 - heads)))], axis=1
    )
    d_from_one, d_norm_gain = pull_one(contract_cols(d_proj_b, w_in))
    grad_tokens = (d_hidden_one + d_from_one).astype(bf16)

    d_beta_rows = tn(d_logits.astype(bf16), xn1)
    parts = [
        (hidden, grad_out, "stack", [(512, 0)] * 2),
        (xn2, d_gate_up, "plain", [(512, 2), (1024, 0)] * 3 + [(512, 2), (512, 0)]),
        (head_out, d_att, "plain", [(1024, 0)]),
        (xn1, d_proj_b[:, :qkv], "plain", [(512, 2), (1024, 0), (1024, 0), (512, 0)]),
    ]
    if own_kernels:
        small = jnp.concatenate(
            [
                d_beta_rows,
                d_norm_gain[None],
                d_mlp_gain[None],
                d_conv.reshape(-1, model),
                jnp.pad(d_head_gain[0:1], ((0, 0), (0, model - width))),
            ],
            axis=0,
        )
        count = small.shape[0]
        small = jnp.pad(small, ((0, -count % 8), (0, 0)))
        (g_down, g_mlp, g_out, g_in), small = scatter_grads(
            (n_dp, n_seq), [(left.T, right, kind, cols) for left, right, kind, cols in parts], small, 2
        )
        mine = (lax.axis_index("dp") * n_seq + lax.axis_index("seq")) * (model // (n_dp * n_seq))
        g_beta = lax.dynamic_slice(small[:heads], (0, mine), (heads, model // (n_dp * n_seq))).T
        s_norm, s_mlp = small[heads], small[heads + 1]
        s_conv = small[heads + 2 : count - 1].reshape(taps_n, qkv)
        s_head = small[count - 1, :width]
    else:
        g_down, g_mlp, g_out, g_in, g_beta = (
            lax.psum_scatter(grad, both, scatter_dimension=0, tiled=True)
            for grad in [contract_rows(left, right) for left, right, _, _ in parts] + [d_beta_rows.T]
        )
        s_norm, s_conv, s_head, s_mlp = lax.psum((d_norm_gain, d_conv, d_head_gain[0], d_mlp_gain), both)
    return (out, grad_tokens, s_norm, g_in, g_beta, s_conv, s_head, g_out, s_mlp, g_mlp, g_down)


def solution(mesh):
    split = P(("dp", "seq"), None)
    placed = (split, P("dp", None), P(), split, split, P(), P(), split, P(), split, split, split)
    return jax.shard_map(
        functools.partial(local, mesh.shape["dp"], mesh.shape["seq"]),
        mesh=mesh,
        in_specs=placed,
        out_specs=(split, split, P(), split, split, P(), P(), split, P(), split, split),
        check_vma=False,
    )
```

profile of v0, /device:TPU:0, one launch (start us, length us, event | category | flops | bytes accessed | tf_op | source)
XLA Modules:
  0.0 501.6 jit_solution(17132467860717991786)
XLA Ops:
  7.9 0.7 convert_element_type.67
  8.6 0.8 copy.70
  9.4 1.6 fusion.22.shard
  11.0 42.4 %gather_rows.1 = bf16[32,32,3200]{2,1,0:T(8,128)(2,1)} custom-call(bf16[32,3200]{1,0:T(8,128)(2,1)} %fusion.22.shard), custom_call_target="tpu_custom_call" | custom-call | tf_op jit(solution)/shard_map/gather_rows/pallas_call | solution.py:617
  53.8 6.4 %fusion.33.refs_2_.refs_3_.refs_4_.pq.pk.pv = f32[512,3200]{1,0:T(8,128)S(1)} fusion(bf16[1024,3200]{1,0:T(8,128)(2,1)} %bitcast.51, bf16[512,1024]{1,0:T(8,128)(2,1)S(1)} %copy-done.5, f32[1024]{0:T(1024)S(1)} %convert_element_type.67, f32[512]{0:T(512)S(1)} %fusion.23), kind=kOutput, calls=%fused_computation.79 | convolution fusion | flops 3357540352 | bytes 14161920 | tf_op jit(solution)/shard_map/dot_general | solution.py:19
  60.2 2.7 copy-done
  62.9 2.4 collective-permute-start
  67.1 1.7 slice.76.refs_14_.logits
  69.1 0.7 convert_element_type.70.refs_11_.aux
  69.8 0.9 copy.72.refs_12_.docs_c
  71.4 80.8 %delta_local.1 = (f32[512,1024]{1,0:T(8,128)}, f32[512,1024]{1,0:T(8,128)}, f32[512,1024]{1,0:T(8,128)}, f32[512,1024]{1,0:T(8,128)}, f32[512,1024]{1,0:T(8,128)...) custom-call(bf16[32,1024]{1,0:T(8,128)(2,1)} %refs_0_.1, ...), custom_call_target="tpu_custom_call" | custom-call | tf_op jit(solution)/shard_map/delta_local/pallas_call | solution.py:725
  152.1 3.5 relay.1.zin
  155.6 10.2 %delta_out.1 = (f32[512,1024]{1,0:T(8,128)}, f32[512,1024]{1,0:T(8,128)}, bf16[512,1024]{1,0:T(8,128)(2,1)}) custom-call(bf16[8,128,128]{2,1,0:T(8,128)(2,1)} %relay.1.zin, f32[512,1024]{1,0:T(8,128)} %get-tuple-element.52.dt.dt_r, f32[512,1024]{1,0:T(8,128)} %get-tuple-element.53.ft, f32[512,1024]{1,0:T(8,128)} %get-tuple-element.54.qt, ...), custom_call_target="tpu_custom_call" | custom-call | tf_op jit(solution)/shard_map/delta_out/pallas_call | solution.py:760
  165.8 2.3 copy.75
  168.1 3.3 multiply_reduce_fusion.2
  171.5 13.4 %fusion.29 = f32[512,5632]{1,0:T(8,128)} fusion(bf16[1024,5632]{1,0:T(8,128)(2,1)} %all-gather.2.cloned.1.call-done, f32[512,1024]{1,0:T(8,128)S(1)} %get-tuple-element.111, f32[1024]{0:T(1024)S(1)} %convert_element_type.71, f32[512]{0:T(512)S(1)} %fusion.24), kind=kOutput, calls=%fused_computation.76 | convolution fusion | flops 5907152896 | bytes 25171968 | tf_op jit(solution)/shard_map/dot_general | solution.py:19
  184.9 12.5 %bitcast_multiply_fusion.1 = (f32[512,2816]{1,0:T(8,128)}, f32[512,2816]{1,0:T(8,128)}, bf16[512,2816]{1,0:T(8,128)(2,1)S(1)}) fusion(f32[512,5632]{1,0:T(8,128)} %fusion.29, bf16[2816,1024]{1,0:T(8,128)(2,1)} %bitcast.63, bf16[512,1024]{1,0:T(8,128)(2,1)S(1)} %copy-done.2), kind=kOutput, calls=%fused_computation.9 | convolution fusion | flops 2972975104 | bytes 32768000 | tf_op jit(solution)/shard_map/dot_general | solution.py:23
  197.4 4.1 add_convert_fusion.1
  201.6 7.4 %add_convert_fusion.refs_5_ = bf16[512,5632]{1,0:T(8,128)(2,1)} fusion(f32[512,2816]{1,0:T(8,128)} %get-tuple-element.94, f32[512,2816]{1,0:T(8,128)} %get-tuple-element.93), kind=kLoop, calls=%fused_computation | loop fusion | flops 5767168 | bytes 17301504 | tf_op jit(solution)/shard_map/convert_element_type | solution.py:780
  208.9 25.0 %multiply_reduce_fusion = (f32[1024]{0:T(1024)S(1)}, f32[512]{0:T(512)S(1)}, f32[512,1024]{1,0:T(8,128)S(1)}) fusion(f32[512,1024]{1,0:T(8,128)S(1)} %get-tuple-element.111, f32[512]{0:T(512)S(1)} %fusion.24, f32[1024]{0:T(1024)S(1)} %convert_element_type.71, bf16[512,5632]{1,0:T(8,128)(2,1)} %add_convert_fusion.refs_5_, ...), kind=kOutput, calls=%fused_computation.34 | convolution fusion | flops 5908724224 | bytes 21508096 | tf_op jit(solution)/shard_map/dot_general | solution.py:23
  234.5 0.7 copy-done.3
  235.2 1.0 copy-done.14
  236.3 2.6 fusion.38.dh
  238.9 10.7 %delta_seed.1 = (f32[512,1024]{1,0:T(8,128)}, f32[512,1024]{1,0:T(8,128)}, f32[8,128,128]{2,1,0:T(8,128)}, f32[8,128]{1,0:T(8,128)}) custom-call(f32[512,1024]{1,0:T(8,128)} %fusion.38.dh, f32[512,1024]{1,0:T(8,128)} %get-tuple-element.68.o, f32[1,128]{1,0:T(1,128)} %bitcast_convert_fusion.gain, f32[512,1024]{1,0:T(8,128)} %get-tuple-element.54.qt, ...), custom_call_target="tpu_custom_call" | custom-call | tf_op jit(solution)/shard_map/delta_seed/pallas_call | solution.py:786
  249.6 31.1 %relay_back.1.g_r = bf16[8,128,128]{2,1,0:T(8,128)(2,1)} custom-call(f32[8,128,128]{2,1,0:T(8,128)} %get-tuple-element.71.map_ref, f32[8,128,128]{2,1,0:T(8,128)} %get-tuple-element.72.add_ref), custom_call_target="tpu_custom_call" | custom-call | tf_op jit(solution)/shard_map/relay_back/pallas_call | solution.py:744
  280.7 31.5 %delta_back.1 = (f32[512,1024]{1,0:T(8,128)}, f32[512,1024]{1,0:T(8,128)}, f32[512,1024]{1,0:T(8,128)}, f32[8,1024]{1,0:T(8,128)}, f32[8,1024]{1,0:T(8,128)}, /*...) custom-call(f32[512,3200]{1,0:T(8,128)} %copy-done, ...), custom_call_target="tpu_custom_call" | custom-call | tf_op jit(solution)/shard_map/delta_back/pallas_call | solution.py:796
  312.3 0.8 convert.21
  313.1 0.8 convert.22
  313.8 0.8 convert.23
  314.6 1.3 collective-permute-start.1
  315.9 1.0 convert_element_type.79
  316.9 0.8 pad_maximum_fusion
  318.1 0.7 slice.69
  318.8 4.6 copy.76.refs_0_
  323.4 3.8 fusion.1.refs_7_
  327.2 9.2 %fusion.14 = (f32[1024]{0:T(1024)S(1)}, f32[512]{0:T(512)S(1)}, f32[512,1024]{1,0:T(8,128)}) fusion(bf16[512,1024]{1,0:T(8,128)(2,1)S(1)} %copy-done.7, f32[512]{0:T(512)S(1)} %fusion.23, f32[1024]{0:T(1024)S(1)} %convert_element_type.67, bf16[1024,3200]{1,0:T(8,128)(2,1)} %bitcast.52, bf16[512,8]{1,0:T(8,128)(2,1)S(1)} %convert_element_type.79, ...), kind=kOutput, calls=%fused_computation.28 | convolution fusion | flops 3368942080 | bytes 12865536 | tf_op jit(solution)/shard_map/dot_general | solution.py:23
  337.3 4.4 fusion.28
  341.8 2.4 copy.77.refs_1_
  344.1 1.3 copy.78.refs_3_
  345.5 137.4 %scatter_grads.1 = (f32[88,1024]{1,0:T(8,128)}, f32[32,5632]{1,0:T(8,128)}, f32[32,1024]{1,0:T(8,128)}, f32[32,3072]{1,0:T(8,128)}, f32[24,1024]{1,0:T(8,128)}) custom-call(bf16[2816,512]{1,0:T(8,128)(2,1)} %copy.76.refs_0_, bf16[1024,512]{1,0:T(8,128)(2,1)} %copy.77.refs_1_, bf16[1024,512]{1,0:T(8,128)(2,1)} %bitcast.53, bf16[1024,512]{1,0:T(8,128)(2,1)} %copy.78.refs_3_, ...), custom_call_target="tpu_custom_call" | custom-call | tf_op jit(solution)/shard_map/scatter_grads/pallas_call | solution.py:496
  482.9 1.2 slice_bitcast_fusion.1
  484.1 1.4 fusion.36
  485.6 0.8 slice.71
  486.3 0.8 slice.72
  488.5 1.8 copy.84
  490.3 1.6 copy.85
  491.8 2.0 copy.86
  493.8 0.7 copy.87
  (75 shorter events, 7.1 us)
Async XLA Ops:
  7.2 164.2 %all-gather.2.cloned.1.call-start = ((), (), s32[]{:S(2)}) async-start(), calls=%async_computation | async-start | bytes 11894784 | tf_op jit(solution)/shard_map/all_gather | solution.py:672
  11.0 42.4 %copy-start.5 = (bf16[512,1024]{1,0:T(8,128)(2,1)S(1)}, bf16[512,1024]{1,0:T(8,128)(2,1)}, u32[]{:S(2)}) copy-start(bf16[512,1024]{1,0:T(8,128)(2,1)} %param.12) | copy-start | bytes 3145732
  53.7 11.6 %copy-start.15 = (s32[1,3]{1,0:T(1,128)S(1)}, s32[1,3]{1,0:T(1,128)}, u32[]{:S(2)}) copy-start(s32[1,3]{1,0:T(1,128)} %param.13) | copy-start | bytes 40
  53.7 12.2 %copy-start.12 = (bf16[4,3072]{1,0:T(4,128)(2,1)S(1)}, bf16[4,3072]{1,0:T(4,128)(2,1)}, u32[]{:S(2)}) copy-start(bf16[4,3072]{1,0:T(4,128)(2,1)} %param.17) | copy-start | bytes 73732
  53.7 12.9 %copy-start.16 = (bf16[128]{0:T(256)(128)(2,1)S(1)}, bf16[128]{0:T(256)(128)(2,1)}, u32[]{:S(2)}) copy-start(bf16[128]{0:T(256)(128)(2,1)} %param.18) | copy-start | bytes 772
  53.8 15.1 %copy-start.13 = (bf16[1024]{0:T(1024)(128)(2,1)S(1)}, bf16[1024]{0:T(1024)(128)(2,1)}, u32[]{:S(2)}) copy-start(bf16[1024]{0:T(1024)(128)(2,1)} %param.20) | copy-start | bytes 6148
  60.2 2.7 copy-start
  62.9 7.7 %collective-permute-start = (bf16[3,3072]{1,0:T(4,128)(2,1)S(1)}, bf16[3,3072]{1,0:T(4,128)(2,1)S(1)}, u32[]{:S(2)}, u32[]{:S(2)}) collective-permute-start(bf16[3,3072]{1,0:T(4,128)(2,1)S(1)} %slice.102), channel_id=1, source_target_pairs={{0,1},{1,2},{2,3},{3,4},{4,5},{5,6},{6,7},{8,9},{9,10},{10,11},{11... | collective-permute-start | bytes 55304 | tf_op jit(solution)/shard_map/ppermute | solution.py:632
  65.7 5.7 %copy-start.11 = (s32[512]{0:T(512)}, s32[512]{0:T(512)S(1)}, u32[]{:S(2)}) copy-start(s32[512]{0:T(512)S(1)} %get-tuple-element.101) | copy-start | bytes 6148
  171.4 13.5 %copy-start.2 = (bf16[512,1024]{1,0:T(8,128)(2,1)S(1)}, bf16[512,1024]{1,0:T(8,128)(2,1)}, u32[]{:S(2)}) copy-start(bf16[512,1024]{1,0:T(8,128)(2,1)} %refs_4_.1) | copy-start | bytes 3145732
  171.4 26.0 %slice-start = ((s8[5767168]{0:T(1024)(128)(4,1)}), s8[4194304]{0:T(1024)(128)(4,1)S(1)}, s32[]{:S(2)}) async-start(s8[5767168]{0:T(1024)(128)(4,1)} %bitcast.64), calls=%async_computation.1 | async-start | bytes 8388608
  184.9 12.5 %slice-start.1 = ((s8[5767168]{0:T(1024)(128)(4,1)}), s8[1572864]{0:T(1024)(128)(4,1)S(1)}, s32[]{:S(2)}) async-start(s8[5767168]{0:T(1024)(128)(4,1)} %bitcast.64), calls=%async_computation.2 | async-start | bytes 3145728
  197.4 4.2 copy-start.9
  233.9 1.3 copy-start.3
  233.9 2.3 copy-start.14
  236.3 2.6 copy-start.4
  280.7 36.9 %copy-start.6 = (bf16[512,1024]{1,0:T(8,128)(2,1)S(1)}, bf16[512,1024]{1,0:T(8,128)(2,1)}, u32[]{:S(2)}) copy-start(bf16[512,1024]{1,0:T(8,128)(2,1)} %param.12) | copy-start | bytes 3145732
  314.6 8.8 %collective-permute-start.1 = (bf16[3,3072]{1,0:T(4,128)(2,1)S(1)}, bf16[3,3072]{1,0:T(4,128)(2,1)S(1)}, u32[]{:S(2)}, u32[]{:S(2)}) collective-permute-start(bf16[3,3072]{1,0:T(4,128)(2,1)S(1)} %pad_maximum_fusion.2), channel_id=1, source_target_pairs={{1,0},{2,1},{3,2},{4,3},{5,4},{6,5},{7,6},{9,8},{10,9},{11,10},{12... | collective-permute-start | bytes 55304 | tf_op jit(solution)/shard_map/ppermute | solution.py:632
  323.4 3.8 copy-start.7
  327.2 9.2 %copy-start.1 = (bf16[512,3072]{1,0:T(8,128)(2,1)}, bf16[512,3072]{1,0:T(8,128)(2,1)S(1)}, u32[]{:S(2)}) copy-start(bf16[512,3072]{1,0:T(8,128)(2,1)S(1)} %fusion.1.refs_7_) | copy-start | bytes 9437188
  341.7 2.4 copy-start.8
  482.9 11.0 %copy-start.10 = (f32[88,1024]{1,0:T(8,128)S(1)}, f32[88,1024]{1,0:T(8,128)}, u32[]{:S(2)}) copy-start(f32[88,1024]{1,0:T(8,128)} %get-tuple-element.137) | copy-start | bytes 1081348
Sparse Core Ops, SparseCore 0:
  10.9 115.9 all-gather.1
where the time goes:
time: 503 us; the launch traced here: 502 us
  Pallas kernels  348 us (69%)
  matrix products  76.9 us (15%)
  local copies, waits for them, and re-layouts  32.2 us (6%)
  other arithmetic  25.8 us (5%)
  between operations  14.6 us (3%)
    pallas_call x1, Pallas kernels, scatter_grads(): pl.pallas_call(functools.partial(scatter_kernel, n_dp, n_seq, units, slot...  137 us
    pallas_call x1, Pallas kernels, local(): pl.pallas_call(functools.partial(local_kernel, sizes, chunk, len(beside))...  80.8 us
    dot_general x4, matrix products, nt(): lax.dot_general(a, b, (((1,), (1,)), ((), ())), precision=prec, preferred...  49.3 us
    pallas_call x1, Pallas kernels, gather_rows(): pl.pallas_call(functools.partial(gather_kernel, sizes), in_specs=[anywher...  42.4 us
    pallas_call x2, Pallas kernels, relay(): pl.pallas_call(functools.partial(relay_kernel, n_seq, back), in_specs=[pl...  34.6 us
    pallas_call x1, Pallas kernels, local(): pl.pallas_call(functools.partial(back_kernel, chunk), grid=(heads,), in_s...  31.5 us
    dot_general x4, matrix products, nn(): lax.dot_general(a, b, (((1,), (0,)), ((), ())), precision=prec, preferred...  27.3 us
    unnamed x43, local copies, waits for them, and re-layouts  11.4 us
  transfers between devices with their start and end apart: 3, of which 0 were waited for; matrix products, arithmetic and copies ran while one was open for 6% of the time, Pallas kernels for 27%

commit v1 on v0

--- a/solution.py
+++ b/solution.py
@@ -13,6 +13,11 @@
 f32, bf16 = jnp.float32, jnp.bfloat16
 HIGH = lax.Precision.HIGH
 VMEM_LIMIT = 56 << 20
+RINGED = 1
+B_COLS = [(1024, 0), (1024, 0), (512, 2), (1024, 0), (512, 2), (1024, 0), (512, 0)]
+B_ORDER = [2, 3, 4, 0, 5, 6, 1, 7, 9, 8]
+TOKEN_TURN = 1
+F_COLS = [[(1024, 0)], [(512, 2), (512, 0)], [(512, 0), (512, 0)]]
 
 
 def nn(a, b, prec=None):
@@ -87,7 +92,8 @@
 ):
     head = pl.program_id(0)
     pad = rest[gathers]
-    gather_beside(sizes, head, shards, rest[:gathers], rest[gathers + 1 :])
+    turns = (0, 1, 5)
+    gather_beside(sizes, head, shards, rest[:gathers], rest[gathers + 1 :], turns)
     rows, width = pq.shape
     keeps = (aux[:, 2:3], aux[:, 3:4], aux[:, 4:5])
     acts = []
@@ -125,12 +131,12 @@
         cc = cont[sl]
         dt = jnp.where(d_row == d_col, cc[chunk - 1 : chunk], 0.0) - xs[c][:, :width]
         ft = xs[c][:, width:]
-        w_o[sl, :] = wus[c][:, :width]
+        w_o[sl, :] = wus[c][:, :width].astype(bf16)
         u_o[sl, :] = wus[c][:, width:]
         qt_o[sl, :] = cc * q[sl] - pwus[c][:, :width]
         o_o[sl, :] = pwus[c][:, width:]
-        t_o[sl, :] = ts[c]
-        p_o[sl, :] = ps[c]
+        t_o[sl, :] = ts[c].astype(bf16)
+        p_o[sl, :] = ps[c].astype(bf16)
         kk_o[sl, :] = kks[c]
         dt_o[c * width : (c + 1) * width, :] = dt
         ft_o[c * width : (c + 1) * width, :] = ft
@@ -142,17 +148,19 @@
     map_o[0] = seg[:, :width]
     turned_o[0] = seg[:, :width].T
     add_o[0] = seg[:, width:]
-
-
-def relay_kernel(n_seq, back, map_ref, add_ref, out_ref, send, ssem, rsem):
-    d, s = lax.axis_index("dp"), lax.axis_index("seq")
-    heads = map_ref.shape[0]
+    gather_rest(sizes, head, shards, rest[:gathers], rest[gathers + 1 :], len(turns), pl.num_programs(0) - 1)
+
+
+def relay_ends(n_seq, back):
+    s = lax.axis_index("seq")
     if back:
-        first, final = s == n_seq - 1, s == 0
-        ahead, behind = s - 1, s + 1
-    else:
-        first, final = s == 0, s == n_seq - 1
-        ahead, behind = s + 1, s - 1
+        return s == n_seq - 1, s == 0, s - 1, s + 1
+    return s == 0, s == n_seq - 1, s + 1, s - 1
+
+
+def relay_greet(n_seq, back):
+    d = lax.axis_index("dp")
+    first, final, ahead, behind = relay_ends(n_seq, back)
     barrier = pltpu.get_barrier_semaphore()
 
     @pl.when(jnp.logical_not(first))
@@ -163,7 +171,18 @@
     def _():
         pl.semaphore_signal(barrier, inc=1, device_id=(d, ahead), device_id_type=MESH)
 
-    pl.semaphore_wait(barrier, jnp.where(first | final, 1, 2))
+    return jnp.where(first | final, 1, 2)
+
+
+def relay_kernel(n_seq, back, *refs):
+    pl.semaphore_wait(pltpu.get_barrier_semaphore(), relay_greet(n_seq, back))
+    relay_body(n_seq, back, *refs)
+
+
+def relay_body(n_seq, back, map_ref, add_ref, out_ref, send, ssem, rsem):
+    d = lax.axis_index("dp")
+    heads = map_ref.shape[0]
+    first, final, ahead, behind = relay_ends(n_seq, back)
 
     def copy_of(h):
         return pltpu.make_async_remote_copy(
@@ -173,35 +192,25 @@
 
     @pl.when(first)
     def _():
-        def start(h, carry):
-            out_ref[h] = jnp.zeros(out_ref.shape[1:], out_ref.dtype)
+        out_ref[...] = jnp.zeros(out_ref.shape, out_ref.dtype)
+        for h in range(heads):
             send[h] = add_ref[h].astype(bf16)
             copy_of(h).start()
-            return carry
-
-        lax.fori_loop(0, heads, start, 0)
 
     @pl.when(jnp.logical_not(first))
     def _():
-        def step(h, carry):
+        for h in range(heads):
             copy_of(h).wait_recv()
+            send[h] = (nn(map_ref[h], out_ref[h].astype(f32), HIGH) + add_ref[h]).astype(bf16)
 
             @pl.when(jnp.logical_not(final))
             def _():
-                send[h] = (nn(map_ref[h], out_ref[h].astype(f32), HIGH) + add_ref[h]).astype(bf16)
                 copy_of(h).start()
-
-            return carry
-
-        lax.fori_loop(0, heads, step, 0)
 
     @pl.when(jnp.logical_not(final))
     def _():
-        def sent(h, carry):
+        for h in range(heads):
             copy_of(h).wait_send()
-            return carry
-
-        lax.fori_loop(0, heads, sent, 0)
 
 
 def output_kernel(chunk, zin, dt, ft, qt, o0, gain, z_o, o_o, head_o):
@@ -210,7 +219,7 @@
     for c in range(rows // chunk):
         sl = slice(c * chunk, (c + 1) * chunk)
         ds = slice(c * width, (c + 1) * width)
-        z_o[ds, :] = z
+        z_o[ds, :] = z.astype(bf16)
         o = o0[sl, :] + nn(qt[sl, :], z, HIGH)
         o_o[sl, :] = o
         scale = lax.rsqrt(jnp.mean(o * o, axis=1, keepdims=True) + norm_eps)
@@ -219,8 +228,11 @@
             z = nn(dt[ds, :], z, HIGH) + ft[ds, :]
 
 
-def seed_kernel(chunk, dh, o, gain, qt, dt, do_o, b_o, seed_o, dgain_o):
-    head = pl.program_id(0)
+def seed_kernel(chunk, *refs):
+    seed_body(chunk, pl.program_id(0), *refs)
+
+
+def seed_body(chunk, head, dh, o, gain, qt, dt, do_o, b_o, seed_o, dgain_o):
     rows, width = qt.shape
     ov, dhv = o[...], dh[...]
     scale = lax.rsqrt(jnp.mean(ov * ov, axis=1, keepdims=True) + norm_eps)
@@ -229,7 +241,7 @@
     dgain_o[...] = jnp.where(head == 0, 0.0, dgain_o[...]) + jnp.broadcast_to(dg, dgain_o.shape)
     y = dhv * gain[...]
     do = (y - n * jnp.mean(y * n, axis=1, keepdims=True)) * scale
-    do_o[...] = do
+    do_o[...] = do.astype(do_o.dtype)
     g = None
     for c in reversed(range(rows // chunk)):
         sl = slice(c * chunk, (c + 1) * chunk)
@@ -239,12 +251,15 @@
     seed_o[0] = g
 
 
-def back_kernel(
-    chunk, pq, pk, pv, hq, hk, hv, tq, tk, tv, aux, docs_c, docs_r, logits,
+def back_kernel(chunk, *refs):
+    back_body(chunk, pl.program_id(0), *refs)
+
+
+def back_body(
+    chunk, head, pq, pk, pv, hq, hk, hv, tq, tk, tv, aux, docs_c, docs_r, logits,
     cq, ck, cv, w_r, u_r, t_r, p_r, kk_r, z_r, do_r, dt_r, b_r, g_r,
-    dpq, dpk, dpv, dhq, dhk, dhv, dtq, dtk, dtv, dlogit_o, pad, mask1, mask2, mask3,
+    dpq, dpk, dpv, dhq, dhk, dhv, dtq, dtk, dtv, dlogit_o, pad, mask1, mask2, mask3, tails=(None,) * 3,
 ):
-    head = pl.program_id(0)
     rows, width = pq.shape
     cont, last = aux[:, 0:1], aux[:, 1:2]
     keeps = (aux[:, 2:3], aux[:, 3:4], aux[:, 4:5])
@@ -256,47 +271,66 @@
     ik = lax.rsqrt(jnp.sum(ak * ak, axis=1, keepdims=True) + unit_eps)
     uq, k = aq * iq, ak * ik
     q = uq * scale
-    g = g_r[0].astype(f32)
-    dqs, dks, dvs, dbs = [], [], [], []
-    for c in reversed(range(rows // chunk)):
-        sl = slice(c * chunk, (c + 1) * chunk)
-        ds = slice(c * width, (c + 1) * width)
-        row, col, same = masks_of(docs_c[sl, :], docs_r[:, sl])
-        qc, kc, vc, bc, cc, lc = q[sl], k[sl], v[sl], beta[sl], cont[sl], last[sl]
-        z = z_r[ds, :]
-        do = do_r[sl, :]
-        wkz = nn(jnp.concatenate([w_r[sl, :], kc], axis=0), z)
-        u = u_r[sl, :] - wkz[:chunk]
-        kz = wkz[chunk:]
-        du = tn(p_r[sl, :], do) + nn(lc * kc, g)
-        dr = tn(t_r[sl, :], du)
-        y = nt(jnp.concatenate([do, dr], axis=0), jnp.concatenate([u, z], axis=0))
-        dp = jnp.where(same & (row >= col), y[:chunk, :chunk], 0.0)
-        da = jnp.where(same & (row > col), -y[chunk:, :chunk], 0.0)
-        bda = bc * da
-        pak = nn(jnp.concatenate([dp, bda], axis=0), kc)
-        dqs.append(cc * y[:chunk, chunk:] + pak[:chunk])
-        dks.append(
-            tn(jnp.concatenate([dp, bda], axis=0), jnp.concatenate([qc, kc], axis=0))
-            + pak[chunk:] + lc * nt(u, g) - (bc * cc) * y[chunk:, chunk:]
-        )
-        dvs.append(bc * dr)
-        dbs.append(
-            jnp.sum(dr * (vc - cc * kz), axis=1, keepdims=True)
+    n_chunk = rows // chunk
+    cuts = [slice(c * chunk, (c + 1) * chunk) for c in range(n_chunk)]
+    blocks = [slice(c * width, (c + 1) * width) for c in range(n_chunk)]
+    gs = [g_r[0].astype(f32)]
+    for c in reversed(range(1, n_chunk)):
+        gs.insert(0, tn(dt_r[blocks[c], :], gs[0]) + b_r[blocks[c], :])
+    row = lax.broadcasted_iota(jnp.int32, (chunk, chunk), 0)
+    col = lax.broadcasted_iota(jnp.int32, (chunk, chunk), 1)
+    same = [docs_c[sl, :] == docs_r[:, sl] for sl in cuts]
+    ks = [k[sl].astype(bf16) for sl in cuts]
+    dos = [do_r[sl, :].astype(bf16) for sl in cuts]
+    zs = [z_r[ds, :].astype(bf16) for ds in blocks]
+    gbs = [g.astype(bf16) for g in gs]
+    wkzs = [
+        nn(jnp.concatenate([w_r[sl, :].astype(bf16), kc], axis=0), z) for sl, kc, z in zip(cuts, ks, zs)
+    ]
+    us = [(u_r[sl, :] - x[:chunk]).astype(bf16) for sl, x in zip(cuts, wkzs)]
+    dus = [tn(p_r[sl, :].astype(bf16), do) for sl, do in zip(cuts, dos)]
+    dus = [x + nn((last[sl] * k[sl]).astype(bf16), g) for x, sl, g in zip(dus, cuts, gbs)]
+    drs = [tn(t_r[sl, :].astype(bf16), x.astype(bf16)) for sl, x in zip(cuts, dus)]
+    ys = [
+        nt(jnp.concatenate([do, dr.astype(bf16)], axis=0), jnp.concatenate([u, z], axis=0))
+        for do, dr, u, z in zip(dos, drs, us, zs)
+    ]
+    dps = [jnp.where(m & (row >= col), y[:chunk, :chunk], 0.0) for m, y in zip(same, ys)]
+    das = [jnp.where(m & (row > col), -y[chunk:, :chunk], 0.0) for m, y in zip(same, ys)]
+    pbs = [
+        jnp.concatenate([dp, beta[sl] * da], axis=0).astype(bf16) for dp, da, sl in zip(dps, das, cuts)
+    ]
+    paks = [nn(pb, kc) for pb, kc in zip(pbs, ks)]
+    turns = [
+        tn(pb, jnp.concatenate([q[sl].astype(bf16), kc], axis=0)) for pb, sl, kc in zip(pbs, cuts, ks)
+    ]
+    ugs = [nt(u, g) for u, g in zip(us, gbs)]
+    dq = jnp.concatenate([cont[sl] * y[:chunk, chunk:] + x[:chunk] for sl, y, x in zip(cuts, ys, paks)], axis=0)
+    dk = jnp.concatenate(
+        [
+            t + x[chunk:] + last[sl] * ug - (beta[sl] * cont[sl]) * y[chunk:, chunk:]
+            for t, x, sl, ug, y in zip(turns, paks, cuts, ugs, ys)
+        ],
+        axis=0,
+    )
+    dv = jnp.concatenate([beta[sl] * dr for sl, dr in zip(cuts, drs)], axis=0)
+    db = jnp.concatenate(
+        [
+            jnp.sum(dr * (v[sl] - cont[sl] * x[chunk:]), axis=1, keepdims=True)
             + jnp.sum(da * kk_r[sl, :], axis=1, keepdims=True)
-        )
-        if c > 0:
-            g = tn(dt_r[ds, :], g) + b_r[ds, :]
-    dq, dk, dv, db = (jnp.concatenate(x[::-1], axis=0) for x in (dqs, dks, dvs, dbs))
+            for dr, sl, x, da in zip(drs, cuts, wkzs, das)
+        ],
+        axis=0,
+    )
     lane = lax.broadcasted_iota(jnp.int32, dlogit_o.shape, 1)
     dlogit_o[...] = jnp.where(lane == head, db * beta * (1.0 - beta), jnp.where(head == 0, 0.0, dlogit_o[...]))
     du_q = dq * scale
     da_q = (du_q - uq * jnp.sum(uq * du_q, axis=1, keepdims=True)) * iq
     da_k = (dk - k * jnp.sum(k * dk, axis=1, keepdims=True)) * ik
-    for dact, sg, c_r, src, halo, taps, dst, dhalo, dtaps in (
-        (da_q, sq, cq, pq, hq, tq, dpq, dhq, dtq),
-        (da_k, sk, ck, pk, hk, tk, dpk, dhk, dtk),
-        (dv, sv, cv, pv, hv, tv, dpv, dhv, dtv),
+    for dact, sg, c_r, src, halo, taps, dst, dhalo, dtaps, tail in (
+        (da_q, sq, cq, pq, hq, tq, dpq, dhq, dtq, tails[0]),
+        (da_k, sk, ck, pk, hk, tk, dpk, dhk, dtk, tails[1]),
+        (dv, sv, cv, pv, hv, tv, dpv, dhv, dtv, tails[2]),
     ):
         dconv = dact * (sg * (1.0 + c_r[...] * (1.0 - sg)))
         pad[0:8, :] = halo[...]
@@ -314,8 +348,10 @@
             mask[8 + rows : 16 + rows, :] = zero
             total = total + taps[3 - back : 4 - back, :] * mask[8 + back : 8 + back + rows, :]
             early = early + taps[3 - back : 4 - back, :] * mask[back : back + 8, :]
-        dst[...] = total
+        dst[...] = total.astype(dst.dtype)
         dhalo[...] = early
+        if tail is not None:
+            tail[...] = total[rows - 16 :]
         dtaps[...] = jnp.concatenate(gtaps + [jnp.zeros((4, width), f32)], axis=0)
 
 
@@ -330,20 +366,16 @@
     )
 
 
-def scatter_kernel(n_dp, n_seq, units, slots, n_left, n_right, n_out, *refs):
-    lefts = refs[:n_left]
-    rights = refs[n_left : n_left + n_right]
-    small_in = refs[n_left + n_right]
-    outs = refs[n_left + n_right + 1 : n_left + n_right + 1 + n_out]
-    small_out = refs[n_left + n_right + 1 + n_out]
-    scratch = list(refs[n_left + n_right + 2 + n_out :])
+def scatter_steps(sizes, units, slots, lefts, rights, outs, scratch):
+    n_dp, n_seq = sizes
+    scratch = list(scratch)
     orders = bit_orders(n_dp, n_seq)
     steps = len(orders[0])
     pool = [scratch.pop(0) for _ in range(2 * (1 + max(slots)))]
     own = [pool[2 * slots[u] + half] for u in range(len(units)) for half in (0, 1)]
     before = [max([w for w in range(u) if slots[w] == slots[u]], default=None) for u in range(len(units))]
     got = [[scratch.pop(0) for _ in range(steps)] for _ in range(2 * len(units))]
-    small_got, ssem, rsem, small_ssem, small_rsem = scratch
+    ssem, rsem = scratch
     index = {"dp": lax.axis_index("dp"), "seq": lax.axis_index("seq")}
 
     def bit_of(axis, bit):
@@ -354,10 +386,12 @@
         other[axis] = index[axis] + (1 - 2 * bit_of(axis, bit)) * 2**bit
         return (other["dp"], other["seq"])
 
-    barrier = pltpu.get_barrier_semaphore()
-    for axis, bit in orders[0]:
-        pl.semaphore_signal(barrier, inc=1, device_id=partner(axis, bit), device_id_type=MESH)
-    pl.semaphore_wait(barrier, steps)
+    def greet():
+        for axis, bit in orders[0]:
+            pl.semaphore_signal(
+                pltpu.get_barrier_semaphore(), inc=1, device_id=partner(axis, bit), device_id_type=MESH
+            )
+        return steps
 
     def weights(order):
         return {key: 2 ** (steps - 1 - i) for i, key in enumerate(order)}
@@ -367,25 +401,28 @@
         return sum(((value // 2**b) % 2) * w[(a, b)] for a, b in order if a == axis)
 
     def compute(u):
-        kind, li, ri, first, cols, _, _, first_order = units[u]
-        left, right = lefts[li], rights[ri]
-        block = left.shape[0] // (n_dp * n_seq)
-        group = block * n_seq
-        for half in (0, 1):
-            order, buf = orders[first_order + half], own[2 * u + half]
-            part = pl.ds(first + half * (cols // 2), cols // 2)
-
-            def rows_of(m, carry):
-                base = place(order, "dp", m)
-                tile = nn(left[pl.ds(pl.multiple_of(m * group, 16), group), :], right[:, part])
-                for j in range(n_seq):
-                    piece = tile[j * block : (j + 1) * block]
+        kind, li, _, _, cols, _, _, first_order = units[u]
+        left, (right, first) = lefts[li], rights(u)
+        block = left.shape[1] // (n_dp * n_seq)
+        together = n_seq
+        while together * block % 128:
+            together *= 2
+        half_cols = cols // 2
+
+        def rows_of(m, carry):
+            span = pl.ds(pl.multiple_of(m * (together * block), 128), together * block)
+            tile = tn(left[:, span], right[:, first : first + cols])
+            for half in (0, 1):
+                order, buf = orders[first_order + half], own[2 * u + half]
+                for j in range(together):
+                    piece = tile[j * block : (j + 1) * block, half * half_cols : (half + 1) * half_cols]
                     if kind == "stack":
                         piece = jnp.concatenate([piece[:, : cols // 4], piece[:, cols // 4 :]], axis=0)
-                    buf[base + place(order, "seq", j)] = piece.astype(bf16)
-                return carry
-
-            lax.fori_loop(0, n_dp, rows_of, 0)
+                    base = place(order, "dp", m * (together // n_seq) + j // n_seq)
+                    buf[base + place(order, "seq", j % n_seq)] = piece.astype(bf16)
+            return carry
+
+        lax.fori_loop(0, n_dp * n_seq // together, rows_of, 0)
 
     def copy_of(u, half, k):
         src = own[2 * u + half] if k == 0 else got[2 * u + half][k - 1]
@@ -407,7 +444,7 @@
         copy_of(u, half, k).wait_recv()
         if k < steps - 1:
             def add(i, carry):
-                dst[i] = (dst[i].astype(f32) + src[mine + i].astype(f32)).astype(bf16)
+                dst[i] = dst[i] + src[mine + i]
                 return carry
 
             lax.fori_loop(0, count, add, 0)
@@ -423,12 +460,37 @@
             else:
                 outs[oi][:, start : start + wide] = total
 
+    def begin(u):
+        if before[u] is not None:
+            for half in (0, 1):
+                copy_of(before[u], half, 0).wait_send()
+        compute(u)
+        for half in (0, 1):
+            copy_of(u, half, 0).start()
+
+    def both_merge(u, k):
+        for half in (0, 1):
+            merge(u, half, k)
+
+    def finish():
+        for k in range(steps):
+            for u in range(len(units)):
+                if k > 0 or u not in before:
+                    for half in (0, 1):
+                        copy_of(u, half, k).wait_send()
+
+    return steps, partner, greet, begin, both_merge, finish
+
+
+def small_steps(sizes, partner, small_in, small_out, small_got, small_ssem, small_rsem):
+    order = bit_orders(*sizes)[0]
+    steps = len(order)
+
     def small_copy(k):
-        axis, bit = orders[0][k]
         return pltpu.make_async_remote_copy(
             src_ref=small_in if k == 0 else small_got.at[steps + k - 1], dst_ref=small_got.at[k],
             send_sem=small_ssem.at[k], recv_sem=small_rsem.at[k],
-            device_id=partner(axis, bit), device_id_type=MESH,
+            device_id=partner(*order[k]), device_id_type=MESH,
         )
 
     def small_step(k):
@@ -440,50 +502,33 @@
         else:
             small_out[...] = small_got[k] + mine
 
-    small_copy(0).start()
-    for t in range(len(units) + steps):
-        if t < len(units):
-            if before[t] is not None:
-                for half in (0, 1):
-                    copy_of(before[t], half, 0).wait_send()
-            compute(t)
-            for half in (0, 1):
-                copy_of(t, half, 0).start()
-        if t < steps:
-            small_step(t)
+    def small_finish():
         for k in range(steps):
-            u = t - 1 - k
-            if 0 <= u < len(units):
-                for half in (0, 1):
-                    merge(u, half, k)
-    for k in range(steps):
-        small_copy(k).wait_send()
-        for u in range(len(units)):
-            if k > 0 or u not in before:
-                for half in (0, 1):
-                    copy_of(u, half, k).wait_send()
-
-
-def scatter_grads(mesh_sizes, products, small, cid):
-    n_dp, n_seq = mesh_sizes
-    n = n_dp * n_seq
-    orders = bit_orders(n_dp, n_seq)
-    steps = len(orders[0])
-    lefts, rights, units, shapes, outs = [], [], [], [], []
+            small_copy(k).wait_send()
+
+    return small_copy(0).start, small_step, small_finish
+
+
+def scatter_layout(sizes, products, order, keep):
+    n = sizes[0] * sizes[1]
+    steps = n.bit_length() - 1
+    units, outs = [], []
     for oi, (left, right, kind, cols) in enumerate(products):
-        block = left.shape[0] // n
-        lefts.append(left)
-        rights.append(right)
+        block = left.shape[1] // n
         outs.append(jax.ShapeDtypeStruct((block, right.shape[1]), f32))
         first = 0
         for wide, first_order in cols:
             units.append((kind, oi, oi, first, wide, oi, first, first_order))
             first += wide
-            shapes.append((2 * block, wide // 4) if kind == "stack" else (block, wide // 2))
+    units = [units[i] for i in order or range(len(units))]
+    shapes = []
+    for kind, oi, _, _, wide, _, _, _ in units:
+        block = outs[oi].shape[0]
+        shapes.append((2 * block, wide // 4) if kind == "stack" else (block, wide // 2))
     pool, slots = [], []
     for u, shape in enumerate(shapes):
         alike = [i for i, kept in enumerate(pool) if kept == shape]
-        if len(alike) < 3:
+        if len(alike) < keep[units[u][0]]:
             slots.append(len(pool))
             pool.append(shape)
         else:
@@ -491,21 +536,221 @@
             slots.append(alike[used.index(min(used))])
     own = [pltpu.VMEM((n,) + s, bf16) for s in pool for _ in (0, 1)]
     got = [pltpu.VMEM((n >> (k + 1),) + s, bf16) for s in shapes for _ in (0, 1) for k in range(steps)]
-    vmem = pl.BlockSpec(memory_space=pltpu.VMEM)
     sems = pltpu.SemaphoreType.DMA((len(units), 2, steps))
-    results = pl.pallas_call(
-        functools.partial(scatter_kernel, n_dp, n_seq, units, slots, len(lefts), len(rights), len(outs)),
-        in_specs=[vmem] * (len(lefts) + len(rights) + 1),
-        out_specs=[vmem] * (len(outs) + 1),
-        out_shape=outs + [jax.ShapeDtypeStruct(small.shape, f32)],
-        scratch_shapes=own + got + [
-            pltpu.VMEM((2 * steps,) + small.shape, f32), sems, sems,
-            pltpu.SemaphoreType.DMA((steps,)), pltpu.SemaphoreType.DMA((steps,)),
-        ],
-        compiler_params=pltpu.CompilerParams(collective_id=cid, has_side_effects=True, vmem_limit_bytes=63 << 20),
-        name="scatter_grads",
-    )(*lefts, *rights, small)
-    return results[:-1], results[-1]
+    return units, slots, outs, own + got + [sems, sems]
+
+
+def back_scatter_kernel(sizes, chunk, heads, units, slots, plan, n_prod, *refs):
+    turn = pl.program_id(0)
+    refs = list(refs)
+
+    def take(count):
+        got = refs[:count]
+        del refs[:count]
+        return got
+
+    far_lefts, far_rights = take(n_prod), take(n_prod)
+    dh, o, gain, qt, dt, turned = take(6)
+    common, saved = take(13), take(9)
+    outs, mains, tapped, tail_o, dlogit, dgain = take(n_prod), take(3), take(3), *take(3)
+    lefts, rights, fetch, ring_sem = take(n_prod), take(n_prod), *take(2)
+    do_s, b_s, seed_s, g_s, send, relay_ssem, relay_rsem = take(7)
+    pads = take(4)
+    early_s, late_s, tail_s, halo_ssem, halo_rsem = take(5)
+    ringed = [u for u, unit in enumerate(units) if unit[1] == RINGED]
+
+    def right_of(u):
+        if u in ringed:
+            return rights[RINGED].at[ringed.index(u) % 2], 0
+        return rights[units[u][2]], units[u][3]
+
+    def ring_fetch(place):
+        _, _, ri, first, wide, _, _, _ = units[ringed[place]]
+        return pltpu.make_async_copy(
+            far_rights[ri].at[:, pl.ds(first, wide)],
+            rights[ri].at[place % 2, :, pl.ds(0, wide)],
+            ring_sem.at[place % 2],
+        )
+
+    steps, partner, greet, begin, merge, finish = scatter_steps(sizes, units, slots, lefts, right_of, outs, refs)
+
+    def fetches(i):
+        copies = [pltpu.make_async_copy(far_lefts[i], lefts[i], fetch.at[i, 0])]
+        if i != RINGED:
+            copies.append(pltpu.make_async_copy(far_rights[i], rights[i], fetch.at[i, 1]))
+        return copies
+
+    segment = lax.axis_index("seq")
+
+    def halo_copy(head):
+        return pltpu.make_async_remote_copy(
+            src_ref=early_s.at[head], dst_ref=late_s.at[head], send_sem=halo_ssem.at[head], recv_sem=halo_rsem.at[head],
+            device_id=(lax.axis_index("dp"), segment - 1), device_id_type=MESH,
+        )
+
+    seen = [unit[1] for unit in units]
+    arrival = sorted(range(n_prod), key=seen.index)
+
+    @pl.when(turn == 0)
+    def _():
+        for i in arrival:
+            for copy in fetches(i):
+                copy.start()
+        for place in (0, 1):
+            ring_fetch(place).start()
+        pl.semaphore_wait(pltpu.get_barrier_semaphore(), greet() + relay_greet(sizes[1], True))
+
+    @pl.when(turn < heads)
+    def _():
+        seed_body(
+            chunk, turn, dh, o, gain, qt, dt, do_s.at[turn], b_s.at[turn], seed_s.at[pl.ds(turn, 1)], dgain
+        )
+
+    @pl.when(turn == heads)
+    def _():
+        relay_body(sizes[1], True, turned, seed_s, g_s, send, relay_ssem, relay_rsem)
+
+    for t, events in enumerate(plan):
+        if events:
+            @pl.when(turn == t)
+            def _(events=events):
+                for u, k in events:
+                    if k < 0:
+                        if seen.index(seen[u]) == u:
+                            for copy in fetches(seen[u]):
+                                copy.wait()
+                        if u in ringed:
+                            ring_fetch(ringed.index(u)).wait()
+                        begin(u)
+                        if u in ringed and ringed.index(u) + 2 < len(ringed):
+                            ring_fetch(ringed.index(u) + 2).start()
+                    else:
+                        merge(u, k)
+
+    @pl.when(turn >= heads)
+    def _():
+        head = turn - heads
+        back_body(
+            chunk, head, *common, *saved, do_s.at[head], dt, b_s.at[head], g_s.at[pl.ds(head, 1)],
+            *mains, *[early_s.at[head, third] for third in range(3)], *tapped, dlogit, *pads,
+            tails=[tail_s.at[head, third] for third in range(3)],
+        )
+
+        @pl.when(segment > 0)
+        def _():
+            halo_copy(head).start()
+
+    @pl.when(turn == 2 * heads - 1)
+    def _():
+        width = late_s.shape[3]
+
+        @pl.when(segment == sizes[1] - 1)
+        def _():
+            late_s[...] = jnp.zeros(late_s.shape, f32)
+
+        @pl.when(segment < sizes[1] - 1)
+        def _():
+            for head in range(heads):
+                halo_copy(head).wait_recv()
+
+        for head in range(heads):
+            for third in range(3):
+                tail = tail_s[head, third]
+                tail = jnp.concatenate([tail[:8], tail[8:] + late_s[head, third]], axis=0)
+                tail_o[:, (third * heads + head) * width : (third * heads + head + 1) * width] = tail.astype(bf16)
+
+        @pl.when(segment > 0)
+        def _():
+            for head in range(heads):
+                halo_copy(head).wait_send()
+
+        finish()
+
+
+def final_kernel(sizes, units, slots, *refs):
+    refs = list(refs)
+
+    def take(count):
+        got = refs[:count]
+        del refs[:count]
+        return got
+
+    far, (far_w, tails, xn1, tokens, d_one, gain, dlogit, small_in) = take(3), take(8)
+    outs, (small_out, grad_o) = take(3), take(2)
+    rights, (weight, small_s, gain_s, fetch) = take(3), take(4)
+    small_scratch = take(3)
+    rows, model = xn1.shape
+    steps, partner, greet, begin, merge, finish = scatter_steps(
+        sizes, units, slots, [xn1] * 3, lambda u: (rights[units[u][2]], units[u][3]), outs, refs
+    )
+    small_start, small_step, small_finish = small_steps(sizes, partner, small_s, small_out, *small_scratch)
+    fetches = [pltpu.make_async_copy(a, b, fetch.at[i]) for i, (a, b) in enumerate(zip(far + [far_w], rights + [weight]))]
+    for copy in fetches:
+        copy.start()
+    pl.semaphore_wait(pltpu.get_barrier_semaphore(), greet())
+    small_s[...] = small_in[...]
+    small_s[0:8, :] = tn(dlogit[...], xn1[...])[0:8]
+
+    def token_grads():
+        part = rows // 2
+        fetches[3].wait()
+        gain_s[...] = jnp.zeros(gain_s.shape, f32)
+
+        def some(i, carry):
+            at = pl.ds(pl.multiple_of(i * part, 16), part)
+            dx = nt(dlogit[at, :], weight[:, 3 * model :])
+            for third in range(3):
+                dx = dx + nt(rights[third][at, :], weight[:, third * model : (third + 1) * model])
+            x = tokens[at, :].astype(f32)
+            scale = lax.rsqrt(jnp.mean(x * x, axis=1, keepdims=True) + norm_eps)
+            n = x * scale
+            gain_s[0:1, :] += jnp.sum(dx * n, axis=0, keepdims=True)
+            y = dx * gain[...]
+            dz = (y - n * jnp.mean(y * n, axis=1, keepdims=True)) * scale
+            grad_o[at, :] = (d_one[at, :] + dz).astype(bf16)
+            return carry
+
+        lax.fori_loop(0, 2, some, 0)
+        small_s[8:9, :] = gain_s[0:1, :]
+
+    seen = [unit[2] for unit in units]
+    for t in range(len(units) + steps):
+        for k in range(steps):
+            if 0 <= t - 1 - k < len(units):
+                merge(t - 1 - k, k)
+        if t < len(units):
+            third = seen[t]
+            if seen.index(third) == t and third not in seen[: TOKEN_TURN + 1][:t] and (t <= TOKEN_TURN):
+                fetches[third].wait()
+                rights[third][rows - 16 :, :] = tails[:, third * model : (third + 1) * model]
+            begin(t)
+        if t == len(units) - 1:
+            small_start()
+        if 0 <= t - len(units) < steps:
+            small_step(t - len(units))
+        if t == TOKEN_TURN:
+            for copy in fetches[max(seen[: t + 1]) + 1 : 3]:
+                copy.wait()
+            for third in range(max(seen[: t + 1]) + 1, 3):
+                rights[third][rows - 16 :, :] = tails[:, third * model : (third + 1) * model]
+            token_grads()
+    finish()
+    small_finish()
+
+
+def back_plan(n_units, steps, heads, early):
+    plan = [[] for _ in range(2 * heads)]
+    for i in range(n_units + steps):
+        turn = 2 * i if i <= early else heads + i - early - 1
+        turn = min(turn, 2 * heads - 1)
+        for k in range(steps):
+            if 0 <= i - 1 - k < n_units and not (i == early + 1 and k == 0):
+                plan[turn].append((i - 1 - k, k))
+        if i < n_units:
+            plan[turn].append((i, -1))
+        if i == early:
+            plan[heads - 1].append((early, 0))
+    return plan
 
 
 def gather_steps(sizes, shard, whole, own_sem, ssem, rsem):
@@ -577,24 +822,36 @@
     finish()
 
 
-def gather_beside(sizes, turn, shards, wholes, sems):
+def gather_beside(sizes, turn, shards, wholes, sems, turns):
     plans = [
         gather_steps(sizes, shard, whole, *sems[3 * i : 3 * i + 3])
         for i, (shard, whole) in enumerate(zip(shards, wholes))
     ]
     if not plans:
         return
-    steps = plans[0][0]
-    for hops in range(steps + 1):
-        @pl.when(turn == hops)
+    greet = plans[0][1]
+    for hops, when in enumerate(turns):
+        @pl.when(turn == when)
         def _(hops=hops):
             if hops == 0:
-                plans[0][1]()
+                greet()
             for plan in plans:
                 plan[2](hops)
 
-    @pl.when(turn == steps + 1)
+
+def gather_rest(sizes, turn, shards, wholes, sems, done, final):
+    plans = [
+        gather_steps(sizes, shard, whole, *sems[3 * i : 3 * i + 3])
+        for i, (shard, whole) in enumerate(zip(shards, wholes))
+    ]
+    if not plans:
+        return
+
+    @pl.when(turn == final)
     def _():
+        for hops in range(done, plans[0][0] + 1):
+            for plan in plans:
+                plan[2](hops)
         for plan in plans:
             plan[3]()
 
@@ -669,14 +926,14 @@
 
     sizes = (n_dp, n_seq)
     own_kernels = (model // (n_dp * n_seq)) % 32 == 0 and heads > (n_dp * n_seq).bit_length()
-    w_m = lax.all_gather(w_mlp_in, both, axis=0, tiled=True)
+    w_d = lax.all_gather(w_down, both, axis=0, tiled=True)
     w_in = jnp.concatenate([w_qkv, jnp.pad(w_beta, ((0, 0), (0, 128 - heads)))], axis=1)
     if own_kernels:
-        beside = [w_out, w_down]
+        beside = [w_out, w_mlp_in]
         w_in = gather_rows(sizes, w_in, 3)
     else:
         beside = []
-        w_in, w_o, w_d = (lax.all_gather(w, both, axis=0, tiled=True) for w in (w_in, w_out, w_down))
+        w_in, w_o, w_m = (lax.all_gather(w, both, axis=0, tiled=True) for w in (w_in, w_out, w_mlp_in))
 
     inputs = tokens.astype(f32)
     norm_one, pull_one = jax.vjp(rms_scale, inputs, norm_gain.astype(f32))
@@ -728,7 +985,8 @@
         in_specs=[anywhere] * len(beside) + common_specs,
         out_specs=[per_head(rows)] * 7 + [chunk_block] * 3 + [per_head(n_chunk * width)] * 2 + [state_block] * 3
         + [anywhere] * len(beside),
-        out_shape=[token_like] * 7 + [chunk_like] * 3 + [state_like] * 2 + [maps_like] * 3
+        out_shape=[token_like] * 3 + [jax.ShapeDtypeStruct((rows, cols), bf16)] + [token_like] * 3
+        + [jax.ShapeDtypeStruct((rows, heads * chunk), bf16)] * 2 + [chunk_like] + [state_like] * 2 + [maps_like] * 3
         + [whole_like(sizes, w) for w in beside],
         scratch_shapes=[pltpu.VMEM((rows + 8, width), f32)] + [sem for _ in beside for sem in gather_sems(sizes)],
         compiler_params=pltpu.CompilerParams(
@@ -738,7 +996,7 @@
         name="delta_local",
     )(*beside, *common)
     if beside:
-        w_o, w_d = (flat_rows(w) for w in wholes)
+        w_o, w_m = (flat_rows(w) for w in wholes)
 
     def relay(back, maps, adds, cid):
         return pl.pallas_call(
@@ -762,7 +1020,9 @@
         grid=(heads,),
         in_specs=[state_block, per_head(n_chunk * width), per_head(n_chunk * width), per_head(rows), per_head(rows), whole((1, width))],
         out_specs=[per_head(n_chunk * width), per_head(rows), per_head(rows)],
-        out_shape=[state_like, token_like, jax.ShapeDtypeStruct((rows, cols), bf16)],
+        out_shape=[
+            jax.ShapeDtypeStruct(state_like.shape, bf16), token_like, jax.ShapeDtypeStruct((rows, cols), bf16)
+        ],
         compiler_params=params,
         name="delta_out",
     )(state_in, dt, ft, qt, o0, gain_h)
@@ -783,51 +1043,72 @@
     d_att = d_hidden_one.astype(bf16)
     d_head = contract_cols(d_att, w_o)
 
-    do, b_s, seed, d_head_gain = pl.pallas_call(
-        functools.partial(seed_kernel, chunk),
-        grid=(heads,),
-        in_specs=[per_head(rows), per_head(rows), whole((1, width)), per_head(rows), per_head(n_chunk * width)],
-        out_specs=[per_head(rows), per_head(n_chunk * width), state_block, whole((8, width))],
-        out_shape=[token_like, state_like, jax.ShapeDtypeStruct((heads, width, width), f32), jax.ShapeDtypeStruct((8, width), f32)],
-        compiler_params=params,
-        name="delta_seed",
-    )(d_head, mixed, gain_h, qt, dt)
-    grad_end = relay(True, seg_turned, seed, 1)
-    outs = pl.pallas_call(
-        functools.partial(back_kernel, chunk),
-        grid=(heads,),
-        in_specs=common_specs + [per_head(rows)] * 5 + [chunk_block] * 3
-        + [per_head(n_chunk * width), per_head(rows), per_head(n_chunk * width), per_head(n_chunk * width), state_block],
-        out_specs=[per_head(rows)] * 3 + [per_head(8)] * 6 + [whole((rows, heads))],
-        out_shape=[token_like] * 3 + [jax.ShapeDtypeStruct((8, cols), f32)] * 6 + [jax.ShapeDtypeStruct((rows, heads), f32)],
-        scratch_shapes=[pltpu.VMEM((rows + 8, width), f32)] + [pltpu.VMEM((rows + 16, width), f32)] * 3,
-        compiler_params=params,
-        name="delta_back",
-    )(*common, cq, ck, cv, w_s, u_s, t_s, p_s, kk_s, z_s, do, dt, b_s, grad_end)
-    d_main = jnp.concatenate(outs[:3], axis=1)
-    d_early = jnp.concatenate(outs[3:6], axis=1)
-    d_conv = jnp.concatenate(outs[6:9], axis=1)[:taps_n]
-    d_logits = outs[9]
-    returned = from_behind(d_early[8 - taps_n + 1 :].astype(bf16), "seq", -1).astype(f32)
-    d_projected = d_main + jnp.pad(returned, ((rows - taps_n + 1, 0), (0, 0)))
-    d_proj_b = jnp.concatenate(
-        [d_projected.astype(bf16), jnp.pad(d_logits.astype(bf16), ((0, 0), (0, 128 - heads)))], axis=1
-    )
-    d_from_one, d_norm_gain = pull_one(contract_cols(d_proj_b, w_in))
-    grad_tokens = (d_hidden_one + d_from_one).astype(bf16)
-
-    d_beta_rows = tn(d_logits.astype(bf16), xn1)
     parts = [
         (hidden, grad_out, "stack", [(512, 0)] * 2),
         (xn2, d_gate_up, "plain", [(512, 2), (1024, 0)] * 3 + [(512, 2), (512, 0)]),
         (head_out, d_att, "plain", [(1024, 0)]),
-        (xn1, d_proj_b[:, :qkv], "plain", [(512, 2), (1024, 0), (1024, 0), (512, 0)]),
     ]
     if own_kernels:
+        parts[1] = parts[1][:3] + (B_COLS,)
+        units, slots, grads_like, scratch = scatter_layout(
+            sizes, parts, B_ORDER, {"plain": 2, "stack": 1}
+        )
+        steps = (n_dp * n_seq).bit_length() - 1
+        plan = back_plan(len(units), steps, heads, 3)
+
+        def late(spec):
+            shape, index = spec.block_shape, spec.index_map
+            return pl.BlockSpec(shape, lambda t: index(jnp.maximum(t - heads, 0)))
+
+        def soon(spec):
+            shape, index = spec.block_shape, spec.index_map
+            return pl.BlockSpec(shape, lambda t: index(jnp.minimum(t, heads - 1)))
+
+        def each(spec):
+            shape, index = spec.block_shape, spec.index_map
+            return pl.BlockSpec(shape, lambda t: index(jnp.where(t < heads, t, t - heads)))
+
+        n_prod = len(parts)
+        results = pl.pallas_call(
+            functools.partial(back_scatter_kernel, sizes, chunk, heads, units, slots, plan, n_prod),
+            grid=(2 * heads,),
+            in_specs=[anywhere] * (2 * n_prod)
+            + [soon(per_head(rows))] * 2 + [whole((1, width)), soon(per_head(rows)), each(per_head(n_chunk * width))]
+            + [whole((heads, width, width))]
+            + [late(spec) for spec in common_specs + [per_head(rows)] * 5 + [chunk_block] * 3 + [per_head(n_chunk * width)]],
+            out_specs=[whole(like.shape) for like in grads_like]
+            + [late(spec) for spec in [per_head(rows)] * 3 + [per_head(8)] * 3]
+            + [whole((16, qkv)), whole((rows, heads)), whole((8, width))],
+            out_shape=grads_like + [jax.ShapeDtypeStruct((rows, cols), bf16)] * 3
+            + [jax.ShapeDtypeStruct((8, cols), f32)] * 3
+            + [jax.ShapeDtypeStruct((16, qkv), bf16), jax.ShapeDtypeStruct((rows, heads), f32), jax.ShapeDtypeStruct((8, width), f32)],
+            scratch_shapes=[pltpu.VMEM(p[0].shape, bf16) for p in parts]
+            + [pltpu.VMEM((2, rows, 1024) if i == RINGED else p[1].shape, bf16) for i, p in enumerate(parts)]
+            + [pltpu.SemaphoreType.DMA((n_prod, 2)), pltpu.SemaphoreType.DMA((2,))]
+            + [
+                pltpu.VMEM((heads, rows, width), bf16), pltpu.VMEM((heads, n_chunk * width, width), f32),
+                pltpu.VMEM((heads, width, width), f32), pltpu.VMEM((heads, width, width), bf16),
+                pltpu.VMEM((heads, width, width), bf16),
+                pltpu.SemaphoreType.DMA((heads,)), pltpu.SemaphoreType.DMA((heads,)),
+            ]
+            + [pltpu.VMEM((rows + 8, width), f32)] + [pltpu.VMEM((rows + 16, width), f32)] * 3
+            + [pltpu.VMEM((heads, 3, 8, width), f32)] * 2 + [pltpu.VMEM((heads, 3, 16, width), f32)]
+            + [pltpu.SemaphoreType.DMA((heads,)), pltpu.SemaphoreType.DMA((heads,))]
+            + scratch,
+            compiler_params=pltpu.CompilerParams(
+                collective_id=1, has_side_effects=True, vmem_limit_bytes=63 << 20, dimension_semantics=("arbitrary",)
+            ),
+            name="back_scatter",
+        )(
+            *[p[0] for p in parts], *[p[1] for p in parts], d_head, mixed, gain_h, qt, dt, seg_turned,
+            *common, cq, ck, cv, w_s, u_s, t_s, p_s, kk_s, z_s,
+        )
+        (g_down, g_mlp, g_out), mains, tapped = results[:n_prod], results[n_prod : n_prod + 3], results[n_prod + 3 : n_prod + 6]
+        tails, d_logits, d_head_gain = results[n_prod + 6 :]
+        d_conv = jnp.concatenate(tapped, axis=1)[:taps_n]
         small = jnp.concatenate(
             [
-                d_beta_rows,
-                d_norm_gain[None],
+                jnp.zeros((9, model), f32),
                 d_mlp_gain[None],
                 d_conv.reshape(-1, model),
                 jnp.pad(d_head_gain[0:1], ((0, 0), (0, model - width))),
@@ -836,18 +1117,69 @@
         )
         count = small.shape[0]
         small = jnp.pad(small, ((0, -count % 8), (0, 0)))
-        (g_down, g_mlp, g_out, g_in), small = scatter_grads(
-            (n_dp, n_seq), [(left.T, right, kind, cols) for left, right, kind, cols in parts], small, 2
-        )
+        parts = [(xn1, main, "plain", cols_in) for main, cols_in in zip(mains, F_COLS)]
+        units, slots, grads_like, scratch = scatter_layout(sizes, parts, None, {"plain": 3})
+        vmem = pl.BlockSpec(memory_space=pltpu.VMEM)
+        *g_in, small, grad_tokens = pl.pallas_call(
+            functools.partial(final_kernel, sizes, units, slots),
+            in_specs=[anywhere] * 4 + [vmem] * 7,
+            out_specs=[vmem] * 5,
+            out_shape=grads_like + [jax.ShapeDtypeStruct(small.shape, f32), jax.ShapeDtypeStruct((rows, model), bf16)],
+            scratch_shapes=[pltpu.VMEM((rows, model), bf16)] * 3 + [pltpu.VMEM(w_in.shape, bf16)]
+            + [pltpu.VMEM(small.shape, f32), pltpu.VMEM((8, model), f32), pltpu.SemaphoreType.DMA((4,))]
+            + [pltpu.VMEM((2 * steps,) + small.shape, f32), pltpu.SemaphoreType.DMA((steps,)), pltpu.SemaphoreType.DMA((steps,))]
+            + scratch,
+            compiler_params=pltpu.CompilerParams(collective_id=2, has_side_effects=True, vmem_limit_bytes=63 << 20),
+            name="final_scatter",
+        )(
+            *mains, w_in, tails, xn1, tokens, d_hidden_one, norm_gain.astype(f32)[None],
+            jnp.pad(d_logits, ((0, 0), (0, 128 - heads))).astype(bf16), small,
+        )
+        g_in = jnp.concatenate(g_in, axis=1)
         mine = (lax.axis_index("dp") * n_seq + lax.axis_index("seq")) * (model // (n_dp * n_seq))
         g_beta = lax.dynamic_slice(small[:heads], (0, mine), (heads, model // (n_dp * n_seq))).T
         s_norm, s_mlp = small[heads], small[heads + 1]
         s_conv = small[heads + 2 : count - 1].reshape(taps_n, qkv)
         s_head = small[count - 1, :width]
     else:
+        do, b_s, seed, d_head_gain = pl.pallas_call(
+            functools.partial(seed_kernel, chunk),
+            grid=(heads,),
+            in_specs=[per_head(rows), per_head(rows), whole((1, width)), per_head(rows), per_head(n_chunk * width)],
+            out_specs=[per_head(rows), per_head(n_chunk * width), state_block, whole((8, width))],
+            out_shape=[token_like, state_like, jax.ShapeDtypeStruct((heads, width, width), f32), jax.ShapeDtypeStruct((8, width), f32)],
+            compiler_params=params,
+            name="delta_seed",
+        )(d_head, mixed, gain_h, qt, dt)
+        grad_end = relay(True, seg_turned, seed, 1)
+        outs = pl.pallas_call(
+            functools.partial(back_kernel, chunk),
+            grid=(heads,),
+            in_specs=common_specs + [per_head(rows)] * 5 + [chunk_block] * 3
+            + [per_head(n_chunk * width), per_head(rows), per_head(n_chunk * width), per_head(n_chunk * width), state_block],
+            out_specs=[per_head(rows)] * 3 + [per_head(8)] * 6 + [whole((rows, heads))],
+            out_shape=[token_like] * 3 + [jax.ShapeDtypeStruct((8, cols), f32)] * 6 + [jax.ShapeDtypeStruct((rows, heads), f32)],
+            scratch_shapes=[pltpu.VMEM((rows + 8, width), f32)] + [pltpu.VMEM((rows + 16, width), f32)] * 3,
+            compiler_params=params,
+            name="delta_back",
+        )(*common, cq, ck, cv, w_s, u_s, t_s, p_s, kk_s, z_s, do, dt, b_s, grad_end)
+        d_main = jnp.concatenate(outs[:3], axis=1)
+        d_early = jnp.concatenate(outs[3:6], axis=1)
+        d_conv = jnp.concatenate(outs[6:9], axis=1)[:taps_n]
+        d_logits = outs[9]
+        returned = from_behind(d_early[8 - taps_n + 1 :].astype(bf16), "seq", -1).astype(f32)
+        d_projected = d_main + jnp.pad(returned, ((rows - taps_n + 1, 0), (0, 0)))
+        d_proj_b = jnp.concatenate(
+            [d_projected.astype(bf16), jnp.pad(d_logits.astype(bf16), ((0, 0), (0, 128 - heads)))], axis=1
+        )
+        d_from_one, d_norm_gain = pull_one(contract_cols(d_proj_b, w_in))
+        grad_tokens = (d_hidden_one + d_from_one).astype(bf16)
+
+        d_beta_rows = tn(d_logits.astype(bf16), xn1)
         g_down, g_mlp, g_out, g_in, g_beta = (
             lax.psum_scatter(grad, both, scatter_dimension=0, tiled=True)
-            for grad in [contract_rows(left, right) for left, right, _, _ in parts] + [d_beta_rows.T]
+            for grad in [contract_rows(left, right) for left, right, _, _ in parts]
+            + [contract_rows(xn1, d_proj_b[:, :qkv]), d_beta_rows.T]
         )
         s_norm, s_conv, s_head, s_mlp = lax.psum((d_norm_gain, d_conv, d_head_gain[0], d_mlp_gain), both)
     return (out, grad_tokens, s_norm, g_in, g_beta, s_conv, s_head, g_out, s_mlp, g_mlp, g_down)

time: 503 us -> 465 us (0.924); the launches traced: 502 us -> 457 us
  matrix products: 76.9 us -> 57 us
  local copies, waits for them, and re-layouts: 32.2 us -> 18.8 us
  other arithmetic: 25.8 us -> 19 us
    pallas_call x2 -> x1, Pallas kernels: 34.6 us -> 3.84 us  [relay(): pl.pallas_call(functools.partial(relay_kernel, n_seq, back), in_specs=[pl...]
    pallas_call x3 -> x2, Pallas kernels: 180 us -> 206 us  [the longest x1 148 us: local(): pl.pallas_call(functools.partial(back_scatter_kernel, sizes, chunk, heads...]
    dot_general x4 -> x3, matrix products: 49.3 us -> 26.3 us  [nt(): lax.dot_general(a, b, (((1,), (1,)), ((), ())), precision=prec, preferred...]
    transpose x3 -> x0, local copies, waits for them, and re-layouts: 8.28 us -> none  [local(): (g_down, g_mlp, g_out, g_in), small = scatter_grads((n_dp, n_seq), [(left...]
  transfers between devices with their start and end apart: 3 -> 2, of which waited for: 0 -> 0; matrix products, arithmetic and copies ran while one was open for 6% -> 7% of each run, Pallas kernels for 27% -> 30%
where the time goes in v1:
time: 465 us; the launch traced here: 457 us
  Pallas kernels  344 us (74%)
  matrix products  57 us (12%)
  other arithmetic  19 us (4%)
  local copies, waits for them, and re-layouts  18.8 us (4%)
  between operations  14.8 us (3%)
    pallas_call x1, Pallas kernels, local(): pl.pallas_call(functools.partial(back_scatter_kernel, sizes, chunk, heads...  148 us
    pallas_call x1, Pallas kernels, local(): pl.pallas_call(functools.partial(local_kernel, sizes, chunk, len(beside))...  79.5 us
    pallas_call x1, Pallas kernels, local(): pl.pallas_call(functools.partial(final_kernel, sizes, units, slots), in_s...  57.7 us
    pallas_call x1, Pallas kernels, gather_rows(): pl.pallas_call(functools.partial(gather_kernel, sizes), in_specs=[anywher...  44.4 us
    dot_general x4, matrix products, nn(): lax.dot_general(a, b, (((1,), (0,)), ((), ())), precision=prec, preferred...  30.7 us
    dot_general x3, matrix products, nt(): lax.dot_general(a, b, (((1,), (1,)), ((), ())), precision=prec, preferred...  26.3 us
    pallas_call x1, Pallas kernels, local(): pl.pallas_call(functools.partial(output_kernel, chunk), grid=(heads,), in...  10.5 us
  transfers between devices with their start and end apart: 2, of which 0 were waited for; matrix products, arithmetic and copies ran while one was open for 7% of the time, Pallas kernels for 30%

profile of v1, /device:TPU:0, one launch (start us, length us, event | category | flops | bytes accessed | tf_op | source)
XLA Modules:
  0.0 456.6 jit_solution(17033005138354060931)
XLA Ops:
  7.2 0.7 all-gather.2.cloned.1.call-update
  7.9 0.7 convert_element_type.55
  8.6 0.8 copy.50
  9.4 1.6 fusion.9.shard
  11.0 44.4 %gather_rows.1 = bf16[32,32,3200]{2,1,0:T(8,128)(2,1)} custom-call(bf16[32,3200]{1,0:T(8,128)(2,1)} %fusion.9.shard), custom_call_target="tpu_custom_call" | custom-call | tf_op jit(solution)/shard_map/gather_rows/pallas_call | solution.py:874
  55.4 0.3 fusion.3
  55.7 0.3 fusion.5.refs_5_
  56.0 6.6 %fusion.15.refs_2_.refs_3_.refs_4_.refs_12_.refs_13_.refs_14_ = f32[512,3200]{1,0:T(8,128)S(1)} fusion(bf16[512,1024]{1,0:T(8,128)(2,1)S(1)} %fusion.5.refs_5_, bf16[1024,3200]{1,0:T(8,128)(2,1)} %bitcast.40), kind=kOutput, calls=%fused_computation.55 | convolution fusion | flops 3355443200 | bytes 14155776 | tf_op jit(solution)/shard_map/dot_general | solution.py:24
  62.7 3.0 copy-done
  65.7 2.2 collective-permute-start
  68.3 0.2 slice_reduce_fusion
  68.6 0.6 pad_convert_fusion.refs_8_.refs_9_.refs_10_.refs_18_.refs_19_.refs_20_
  69.2 0.5 bitcast_convert_fusion.gain.refs_8_
  69.7 1.7 slice.71.refs_14_.refs_24_
  71.7 0.7 convert_element_type.58.refs_11_.refs_21_
  72.4 0.9 copy.52.refs_12_.refs_22_
  73.3 0.7 pad_convert_fusion.1.refs_5_.refs_6_.refs_7_.refs_15_.refs_16_.refs_17_
  73.9 79.5 %delta_local.1 = (f32[512,1024]{1,0:T(8,128)}, f32[512,1024]{1,0:T(8,128)}, f32[512,1024]{1,0:T(8,128)}, bf16[512,1024]{1,0:T(8,128)(2,1)}, f32[512,1024]{1,0:T(...) custom-call(bf16[32,1024]{1,0:T(8,128)(2,1)} %refs_0_.1, ...), custom_call_target="tpu_custom_call" | custom-call | tf_op jit(solution)/shard_map/delta_local/pallas_call | solution.py:982
  153.5 3.8 relay.1.zin
  157.3 10.5 %delta_out.1 = (bf16[512,1024]{1,0:T(8,128)(2,1)}, f32[512,1024]{1,0:T(8,128)}, bf16[512,1024]{1,0:T(8,128)(2,1)}) custom-call(bf16[8,128,128]{2,1,0:T(8,128)(2,1)} %relay.1.zin, f32[512,1024]{1,0:T(8,128)} %get-tuple-element.50.dt.refs_10_, f32[512,1024]{1,0:T(8,128)} %get-tuple-element.51.ft, f32[512,1024]{1,0:T(8,128)} %get-tuple-element.52.qt.refs_9_, ...), custom_call_target="tpu_custom_call" | custom-call | tf_op jit(solution)/shard_map/delta_out/pallas_call | solution.py:1018
  167.8 2.6 multiply_reduce_fusion.2
  170.4 0.2 multiply_convert_fusion.1.refs_1_
  170.7 1.1 copy-done.5
  171.8 13.2 %fusion.16 = f32[512,5632]{1,0:T(8,128)} fusion(bf16[512,1024]{1,0:T(8,128)(2,1)S(1)} %multiply_convert_fusion.1.refs_1_, bf16[1024,5632]{1,0:T(8,128)(2,1)} %bitcast.50), kind=kOutput, calls=%fused_computation.56 | convolution fusion | flops 5905580032 | bytes 24117248 | tf_op jit(solution)/shard_map/dot_general | solution.py:24
  185.0 12.7 %fusion.7 = (f32[512,2816]{1,0:T(8,128)}, f32[512,2816]{1,0:T(8,128)}, bf16[512,2816]{1,0:T(8,128)(2,1)}) fusion(f32[512,5632]{1,0:T(8,128)} %fusion.16, bf16[512,1024]{1,0:T(8,128)(2,1)S(1)} %copy-done.3, bf16[2816,1024]{1,0:T(8,128)(2,1)} %all-gather.2.cloned.1.call-done), kind=kOutput, calls=%fused_computation.20 | convolution fusion | flops 2972975104 | bytes 32768000 | tf_op jit(solution)/shard_map/dot_general | solution.py:28
  197.8 7.4 %add_convert_fusion.refs_4_ = bf16[512,5632]{1,0:T(8,128)(2,1)} fusion(f32[512,2816]{1,0:T(8,128)} %get-tuple-element.90, f32[512,2816]{1,0:T(8,128)} %get-tuple-element.89), kind=kLoop, calls=%fused_computation | loop fusion | flops 5767168 | bytes 17301504 | tf_op jit(solution)/shard_map/convert_element_type | solution.py:1040
  205.1 11.0 %multiply_reduce_fusion = (f32[1024]{0:T(1024)S(1)}, f32[512]{0:T(512)S(1)}, f32[512,1024]{1,0:T(8,128)S(1)}) fusion(f32[512,1024]{1,0:T(8,128)S(1)} %get-tuple-element.104, f32[512]{0:T(512)S(1)} %fusion.10, f32[1024]{0:T(1024)S(1)} %convert_element_type.59, bf16[512,5632]{1,0:T(8,128)(2,1)} %add_convert_fusion.refs_4_, bf16[1024,5632]{1,0:T(8,128)(2,1)} %bitcast.51), kind=kOutput, calls=%fused_computation.15 | convolution fusion | flops 5908724224 | bytes 21508096 | tf_op jit(solution)/shard_map/dot_general | solution.py:28
  216.2 2.0 fusion.11
  218.1 2.6 fusion.17.refs_6_
  220.8 147.9 %back_scatter.1 = (f32[88,1024]{1,0:T(8,128)}, f32[32,5632]{1,0:T(8,128)}, f32[32,1024]{1,0:T(8,128)}, bf16[512,1024]{1,0:T(8,128)(2,1)}, bf16[512,1024]{1,0:T(8...) custom-call(bf16[512,2816]{1,0:T(8,128)(2,1)} %get-tuple-element.91., ...), custom_call_target="tpu_custom_call" | custom-call | tf_op jit(solution)/shard_map/back_scatter/pallas_call | solution.py:1072
  368.7 0.7 slice.64
  369.4 0.8 pad_maximum_fusion.1
  370.3 0.7 pad.44.refs_10_
  371.0 1.0 convert.13
  372.0 0.7 pad.42.refs_9_
  372.6 57.7 %final_scatter.1 = (f32[32,1024]{1,0:T(8,128)}, f32[32,1024]{1,0:T(8,128)}, f32[32,1024]{1,0:T(8,128)}, f32[24,1024]{1,0:T(8,128)}, bf16[512,1024]{1,0:T(8,128)(2,1)}) custom-call(bf16[512,1024]{1,0:T(8,128)(2,1)} %get-tuple-element.68.refs_0_, bf16[512,1024]{1,0:T(8,128)(2,1)} %get-tuple-element.69.refs_1_, bf16[512,1024]{1,0:T(8,128)(2,1)} %get-tuple-element.70.refs_2_, ...), custom_call_target="tpu_custom_call" | custom-call | tf_op jit(solution)/shard_map/final_scatter/pallas_call | solution.py:1123
  430.4 1.2 slice_bitcast_fusion.1
  431.6 1.4 fusion.13
  433.0 0.8 slice.66
  433.8 0.8 slice.67
  434.6 0.7 reshape.126
  435.3 0.7 dynamic-slice_bitcast_fusion
  435.9 1.8 pad_maximum_fusion
  437.7 8.3 %add_convert_fusion.1 = bf16[512,1024]{1,0:T(8,128)(2,1)} fusion(f32[512,1024]{1,0:T(8,128)} %copy-done.2, bf16[512,2816]{1,0:T(8,128)(2,1)} %get-tuple-element.91.refs_0_, bf16[2816,1024]{1,0:T(8,128)(2,1)} %all-gather.2.cloned.1.call-done), kind=kOutput, calls=%fused_computation.17 | convolution fusion | flops 2953838592 | bytes 11796480 | tf_op jit(solution)/shard_map/dot_general | solution.py:24
  446.0 1.0 copy.58
  447.0 0.7 copy.59
  447.7 0.9 copy.60
  448.5 0.7 copy.61
  (62 shorter events, 1.0 us)
Async XLA Ops:
  7.2 177.9 %all-gather.2.cloned.1.call-start = ((), (), s32[]{:S(2)}) async-start(), calls=%async_computation | async-start | bytes 5947392 | tf_op jit(solution)/shard_map/all_gather | solution.py:929
  8.6 47.1 %copy-start.11 = (f32[1024]{0:T(1024)}, f32[1024]{0:T(1024)S(1)}, u32[]{:S(2)}) copy-start(f32[1024]{0:T(1024)S(1)} %convert_element_type.55) | copy-start | bytes 12292
  11.0 44.4 %copy-start.1 = (bf16[512,1024]{1,0:T(8,128)(2,1)S(1)}, bf16[512,1024]{1,0:T(8,128)(2,1)}, u32[]{:S(2)}) copy-start(bf16[512,1024]{1,0:T(8,128)(2,1)} %refs_6_.1) | copy-start | bytes 3145732
  56.0 6.7 %copy-start.6 = (bf16[512,1024]{1,0:T(8,128)(2,1)}, bf16[512,1024]{1,0:T(8,128)(2,1)S(1)}, u32[]{:S(2)}) copy-start(bf16[512,1024]{1,0:T(8,128)(2,1)S(1)} %fusion.5.refs_5_) | copy-start | bytes 3145732
  56.0 11.9 %copy-start.17 = (s32[1,3]{1,0:T(1,128)S(1)}, s32[1,3]{1,0:T(1,128)}, u32[]{:S(2)}) copy-start(s32[1,3]{1,0:T(1,128)} %param.13) | copy-start | bytes 40
  56.0 12.6 %copy-start.13 = (bf16[4,3072]{1,0:T(4,128)(2,1)S(1)}, bf16[4,3072]{1,0:T(4,128)(2,1)}, u32[]{:S(2)}) copy-start(bf16[4,3072]{1,0:T(4,128)(2,1)} %param.17) | copy-start | bytes 73732
  56.0 13.2 %copy-start.18 = (bf16[128]{0:T(256)(128)(2,1)S(1)}, bf16[128]{0:T(256)(128)(2,1)}, u32[]{:S(2)}) copy-start(bf16[128]{0:T(256)(128)(2,1)} %param.18) | copy-start | bytes 772
  56.0 15.4 %copy-start.14 = (bf16[1024]{0:T(1024)(128)(2,1)S(1)}, bf16[1024]{0:T(1024)(128)(2,1)}, u32[]{:S(2)}) copy-start(bf16[1024]{0:T(1024)(128)(2,1)} %param.20) | copy-start | bytes 6148
  62.7 3.0 copy-start
  65.7 7.6 %collective-permute-start = (bf16[3,3072]{1,0:T(4,128)(2,1)S(1)}, bf16[3,3072]{1,0:T(4,128)(2,1)S(1)}, u32[]{:S(2)}, u32[]{:S(2)}) collective-permute-start(bf16[3,3072]{1,0:T(4,128)(2,1)S(1)} %slice.97), channel_id=1, source_target_pairs={{0,1},{1,2},{2,3},{3,4},{4,5},{5,6},{6,7},{8,9},{9,10},{10,11},{11... | collective-permute-start | bytes 55304 | tf_op jit(solution)/shard_map/ppermute | solution.py:889
  68.3 5.7 %copy-start.12 = (s32[512]{0:T(512)}, s32[512]{0:T(512)S(1)}, u32[]{:S(2)}) copy-start(s32[512]{0:T(512)S(1)} %get-tuple-element.94) | copy-start | bytes 6148
  157.3 10.5 %copy-start.15 = (bf16[32,32,1024]{2,1,0:T(8,128)(2,1)S(1)}, bf16[32,32,1024]{2,1,0:T(8,128)(2,1)}, u32[]{:S(2)}) copy-start(bf16[32,32,1024]{2,1,0:T(8,128)(2,1)} %get-tuple-element.55) | copy-start | bytes 6291460
  170.4 45.7 %copy-start.2 = (f32[512,1024]{1,0:T(8,128)}, f32[512,1024]{1,0:T(8,128)S(1)}, u32[]{:S(2)}) copy-start(f32[512,1024]{1,0:T(8,128)S(1)} %get-tuple-element.104) | copy-start | bytes 6291460
  170.7 1.2 copy-start.5
  171.8 13.2 %copy-start.3 = (bf16[512,1024]{1,0:T(8,128)(2,1)S(1)}, bf16[512,1024]{1,0:T(8,128)(2,1)}, u32[]{:S(2)}) copy-start(bf16[512,1024]{1,0:T(8,128)(2,1)} %refs_3_.1) | copy-start | bytes 3145732
  216.2 2.0 copy-start.16
  218.1 2.7 copy-start.4
  437.7 8.3 %copy-start.7 = (bf16[512,1024]{1,0:T(8,128)(2,1)S(1)}, bf16[512,1024]{1,0:T(8,128)(2,1)}, u32[]{:S(2)}) copy-start(bf16[512,1024]{1,0:T(8,128)(2,1)} %get-tuple-element.120) | copy-start | bytes 3145732
  446.0 1.0 copy-start.10
  446.0 1.6 copy-start.8
  446.0 2.5 copy-start.9
Sparse Core Ops, SparseCore 0:
  10.9 78.8 all-gather.1
